TPU v7x, 32 devices: a whole 2x2x4 slice. The times are simulated.
32 devices in a mesh: wide: 8 (over z, y), narrow: 4 (over x, core).
Axes of the slice: x: 2, y: 2, z: 4, core: 2. Of those that a mesh axis runs over, the one named last changes fastest.
Arguments:
- chemical_fractions: float32 [53, 16, 32, 128], P(None, 'wide', 'narrow'), may hold values from 0.1 to 1
- thermal_state: float32 [16, 32, 128], P('wide', 'narrow'), may hold values from 1 to 3
- ignited_stacks: int32 [16, 32], P('wide', 'narrow'), may hold values from 0 to 1, as said below
- spreading_number: float32 [53], replicated, may hold values from 0.02 to 0.15
- natural_exponent_scale: float32 [325], replicated, may hold values from -1 to 1
- arrhenius_energy: float32 [325], replicated, may hold values from 0.5 to 2
- incoming_stoichiometry: int32 [325, 53], replicated, may hold values 0 or 1
- outgoing_stoichiometry: int32 [325, 53], replicated, may hold values 0 or 1
Outputs:
- updated: float32 [53, 16, 32, 128], P(None, 'wide', 'narrow')
Inputs may be any that keep to these rules, and one draw needn't show every extreme that they name: `ignited_stacks`: on each device either 8 or 2 of its columns burn. In every group of devices along narrow, those with 8 burning columns are a quarter of the group and consecutive in index, with wrap-around.
All inputs are finite; a program needn't handle non-finite values.
Results may differ from a plain program's by a relative error of at most 0.0001.
Values sent between devices are 32-bit elements; how exact they have to be, the bound alone decides.
A program may use at most 64 MiB of HBM per device.

v0:
```python
import jax
import jax.numpy as jnp
from jax import lax
from jax.sharding import PartitionSpec as P

BURN_MAX = 8


def extended(block, sides, width):
    for axis, dim in sides:
        count = lax.axis_size(axis)
        forward = [(i, i + 1) for i in range(count - 1)]
        forward.append((count - 1, 0))
        backward = [(target, source) for source, target in forward]
        low = lax.ppermute(
            lax.slice_in_dim(block, block.shape[dim] - width, None, axis=dim), axis, forward
        )
        high = lax.ppermute(lax.slice_in_dim(block, 0, width, axis=dim), axis, backward)
        block = jnp.concatenate([low, block, high], axis=dim)
    return block


def diffuse_padded(padded, coeff):
    centre = padded[:, 1:-1, 1:-1]
    beside = padded[:, 2:, 1:-1] + padded[:, :-2, 1:-1]
    beside = beside + padded[:, 1:-1, 2:] + padded[:, 1:-1, :-2]
    beside = beside + jnp.roll(centre, -1, 3) + jnp.roll(centre, 1, 3)
    return centre + coeff * (beside - 6.0 * centre)


def react(
    values, enthalpy_output, natural_exponent_scale, arrhenius_energy, react_mat, react_tr, prod_tr
):
    for substep in range(2):
        logs = jnp.log(values)
        expo = (
            natural_exponent_scale[:, None]
            - arrhenius_energy[:, None] / enthalpy_output[None, :]
            + jnp.dot(
                react_mat, logs, precision=lax.Precision.HIGHEST, preferred_element_type=jnp.float32
            )
        )
        rates = jnp.exp(expo)
        gain = jnp.dot(
            prod_tr, rates, precision=lax.Precision.HIGHEST, preferred_element_type=jnp.float32
        )
        loss = jnp.dot(
            react_tr, rates, precision=lax.Precision.HIGHEST, preferred_element_type=jnp.float32
        )
        values = values * (values + 0.5 * gain) / (values + 0.5 * loss)
    return values


def shards(
    chemical_fractions,
    thermal_state,
    ignited_stacks,
    spreading_number,
    natural_exponent_scale,
    arrhenius_energy,
    incoming_stoichiometry,
    outgoing_stoichiometry,
):
    coeff = spreading_number[:, None, None, None]
    fields = chemical_fractions
    padded = extended(fields, (("wide", 1), ("narrow", 2)), 2)
    fields = diffuse_padded(diffuse_padded(padded, coeff), coeff)
    nspec, cols_x, cols_y, mesh_volumes = fields.shape
    stack_total = cols_x * cols_y
    flat = fields.reshape(nspec, stack_total, mesh_volumes)
    enthalpy_output = thermal_state.reshape(stack_total, mesh_volumes)
    marks = ignited_stacks.reshape(stack_total)
    ranks = jnp.cumsum(marks) - 1
    count = jnp.sum(marks)
    react_mat = incoming_stoichiometry.astype(jnp.float32)
    react_tr = react_mat.T
    prod_tr = outgoing_stoichiometry.astype(jnp.float32).T
    inside = (marks == 1) & (ranks >= 0) & (ranks < 0 + BURN_MAX)
    target = jnp.where(inside, ranks - 0, BURN_MAX)
    index = (
        jnp.zeros((BURN_MAX + 1,), jnp.int32)
        .at[target]
        .set(jnp.arange(stack_total, dtype=jnp.int32))[:BURN_MAX]
    )
    valid = jnp.arange(BURN_MAX, dtype=jnp.int32) < count - 0
    index, valid = (index, valid)
    block_y = jnp.take(flat, index, axis=1)
    width = block_y.shape[1]
    out = react(
        block_y.reshape(nspec, -1),
        jnp.take(enthalpy_output, index, axis=0).reshape(-1),
        natural_exponent_scale,
        arrhenius_energy,
        react_mat,
        react_tr,
        prod_tr,
    )
    result = out.reshape(nspec, width, mesh_volumes)
    spot = jnp.where(valid, index, stack_total)
    flat = flat.at[:, spot].set(result, mode="drop")
    return flat.reshape(nspec, cols_x, cols_y, mesh_volumes)


def solution(mesh):
    in_specs = (
        P(None, "wide", "narrow", None),
        P("wide", "narrow", None),
        P("wide", "narrow"),
        P(),
        P(),
        P(),
        P(),
        P(),
    )
    out_specs = P(None, "wide", "narrow", None)
    return jax.shard_map(shards, mesh=mesh, in_specs=in_specs, out_specs=out_specs, check_vma=False)
```

profile of v0, /device:TPU:0, one launch (start us, length us, event | category | flops | bytes accessed | tf_op | source)
XLA Modules:
  0.0 48.6 jit_solution(657427247053506624)
XLA Ops:
  0.0 1.2 %copy.21 = f32[53,2,8,128]{3,0,2,1:T(8,128)S(1)} copy(f32[53,2,8,128]{3,2,1,0:T(8,128)} %param.8) | data formatting | bytes 868352 | tf_op args[0]
  1.2 3.0 %collective-permute-start = (f32[53,2,8,128]{3,0,2,1:T(8,128)S(1)}, f32[53,2,8,128]{3,0,2,1:T(8,128)S(1)}, u32[]{:S(2)}, u32[]{:S(2)}) collective-permute-start(f32[53,2,8,128]{3,0,2,1:T(8,128)S(1)} %copy.21), channel_id=1, source_target_pairs={{0,4},{4,8},{8,12},{12,16},{16,20},{20,24},{24,28},{28,0},{1,5},{5... | collective-permute-start | bytes 1302536 | tf_op jit(solution)/shard_map/ppermute | solution.py:15
  4.3 3.1 %collective-permute-start.1 = (f32[53,2,8,128]{3,0,2,1:T(8,128)S(1)}, f32[53,2,8,128]{3,0,2,1:T(8,128)S(1)}, u32[]{:S(2)}, u32[]{:S(2)}) collective-permute-start(f32[53,2,8,128]{3,0,2,1:T(8,128)S(1)} %copy.21), channel_id=1, source_target_pairs={{4,0},{8,4},{12,8},{16,12},{20,16},{24,20},{28,24},{0,28},{5,1},{9... | collective-permute-start | bytes 1302536 | tf_op jit(solution)/shard_map/ppermute | solution.py:18
  7.4 0.8 %reshape.120 = s32[16,1]{1,0:T(8,128)S(1)} reshape(s32[2,8]{1,0:T(2,128)} %param.10) | data formatting | bytes 128 | tf_op jit(solution)/shard_map/reshape | solution.py:72
  8.1 1.3 %reduce_sum.9 = s32[]{:T(128)} reduce(s32[2,8]{1,0:T(2,128)} %param.10, s32[]{:T(128)} %constant.17.clone.1), dimensions={0,1}, to_apply=%region_0.1 | reduce | flops 15 | bytes 72 | tf_op jit(solution)/shard_map/reduce_sum | solution.py:74
  9.6 0.6 %scatter_custom_fusion = s32[9]{0:T(128)S(1)} fusion(s32[16]{0:T(128)S(1)} %fusion.39, s32[16]{0:T(128)S(1)} %iota.7, s32[]{:T(128)} %constant.17.clone.1), kind=kCustom, calls=%fused_computation.70 | custom fusion | bytes 40 | tf_op jit(solution)/shard_map/scatter | solution.py:83
  10.3 0.6 %compare_select_fusion.2 = s32[8]{0:T(128)S(1)} fusion(s32[9]{0:T(128)S(1)} %scatter_custom_fusion, s32[]{:T(128)} %reduce_sum.9), kind=kLoop, calls=%fused_computation.66 | loop fusion | flops 40 | bytes 68 | tf_op jit(solution)/shard_map/select_n | solution.py:100
  11.0 12.9 %collective-permute-done = f32[53,2,8,128]{3,0,2,1:T(8,128)S(1)} collective-permute-done((f32[53,2,8,128]{3,0,2,1:T(8,128)S(1)}, f32[53,2,8,128]{3,0,2,1:T(8,128)S(1)}, u32[]{:S(2)}, u32[]{:S(2)}) %collective-permute-start) | collective-permute-done | bytes 434208 | tf_op jit(solution)/shard_map/ppermute | solution.py:15
  24.0 2.0 %collective-permute-done.1 = f32[53,2,8,128]{3,0,2,1:T(8,128)S(1)} collective-permute-done((f32[53,2,8,128]{3,0,2,1:T(8,128)S(1)}, f32[53,2,8,128]{3,0,2,1:T(8,128)S(1)}, u32[]{:S(2)}, u32[]{:S(2)}) %collective-permute-start.1) | collective-permute-done | bytes 434208 | tf_op jit(solution)/shard_map/ppermute | solution.py:18
  26.2 1.7 %collective-permute-start.3 = (f32[53,6,2,128]{3,0,2,1:T(8,128)S(1)}, f32[53,6,2,128]{3,0,2,1:T(8,128)S(1)}, u32[]{:S(2)}, u32[]{:S(2)}) collective-permute-start(f32[53,6,2,128]{3,0,2,1:T(8,128)S(1)} %get-tuple-element.11), channel_id=1, source_target_pairs={{1,0},{2,1},{3,2},{0,3},{5,4},{6,5},{7,6},{4,7},{9,8},{10,9},{11,1... | collective-permute-start | bytes 976904 | tf_op jit(solution)/shard_map/ppermute | solution.py:18
  28.0 0.6 %gather_fusion.1 = f32[8,128]{1,0:T(8,128)S(1)} fusion(f32[16,128]{1,0:T(8,128)S(1)} %bitcast.58, s32[1024]{0:T(1024)S(1)} %pad_clamp_fusion), kind=kCustom, calls=%fused_computation.1 | custom fusion | bytes 8224 | tf_op jit(solution)/shard_map/jit(_take)/gather | solution.py:91
  28.6 6.1 %collective-permute-done.2 = f32[53,6,2,128]{3,0,2,1:T(8,128)S(1)} collective-permute-done((f32[53,6,2,128]{3,0,2,1:T(8,128)S(1)}, f32[53,6,2,128]{3,0,2,1:T(8,128)S(1)}, u32[]{:S(2)}, u32[]{:S(2)}) %collective-permute-start.2) | collective-permute-done | bytes 325664 | tf_op jit(solution)/shard_map/ppermute | solution.py:15
  34.7 0.9 %collective-permute-done.3 = f32[53,6,2,128]{3,0,2,1:T(8,128)S(1)} collective-permute-done((f32[53,6,2,128]{3,0,2,1:T(8,128)S(1)}, f32[53,6,2,128]{3,0,2,1:T(8,128)S(1)}, u32[]{:S(2)}, u32[]{:S(2)}) %collective-permute-start.3) | collective-permute-done | bytes 325664 | tf_op jit(solution)/shard_map/ppermute | solution.py:18
  36.7 1.2 %fusion.21 = f32[53,4,10,128]{3,0,2,1:T(8,128)S(1)} fusion(f32[53,6,8,128]{3,0,2,1:T(8,128)S(1)} %constant_dynamic-update-slice_fusion, f32[53,6,2,128]{3,0,2,1:T(8,128)S(1)} %collective-permute-done.2, f32[53,6,2,128]{3,0,2,1:T(8,128)S(1)} %collective-permute-done.3, f32[53,6,12,128]{3,0,2,1:T(8,128)S(1)} %pad_maximum_fusion, ...), kind=kLoop, calls=%fused_computation.34 | loop fusion | flops 3527680 | bytes 8466644 | tf_op jit(solution)/shard_map/add | solution.py:28
  38.3 0.4 fusion.27
  38.7 0.6 %gather_fusion = f32[8,53,128]{2,1,0:T(8,128)S(1)} fusion(f32[53,16,128]{2,0,1:T(8,128)S(1)} %bitcast.59, s32[1024]{0:T(1024)S(1)} %pad_clamp_fusion), kind=kCustom, calls=%fused_computation | custom fusion | bytes 434208 | tf_op jit(solution)/shard_map/jit(_take)/gather | solution.py:87
  39.6 1.5 %fusion.3 = f32[325,1024]{1,0:T(8,128)S(1)} fusion(f32[1024]{0:T(1024)S(1)} %bitcast_select_fusion, f32[325]{0:T(512)S(1)} %copy-done.5, f32[325]{0:T(512)S(1)} %copy-done.6, f32[53,1024]{1,0:T(8,128)S(1)} %bitcast.62, pred[1024]{0:T(1024)(128)(4,1)S(1)} %broadcast_bitcast_fusion, s32[325,53]{0,1:T(8,128)S(1)} %copy-done.2), kind=kOutput, calls=%fused_computation.10 | convolution fusion | flops 212730688 | bytes 1624908 | tf_op jit(solution)/shard_map/dot_general | solution.py:39
  41.0 1.1 %fusion.9 = f32[53,1024]{1,0:T(8,128)S(1)} fusion(f32[325,1024]{1,0:T(8,128)S(1)} %fusion.3, f32[53,1024]{1,0:T(8,128)S(1)} %bitcast.63, pred[1024]{0:T(1024)(128)(4,1)S(1)} %broadcast_bitcast_fusion, s32[325,53]{0,1:T(8,128)S(1)} %copy-done.2), kind=kOutput, calls=%fused_computation.21 | convolution fusion | flops 211840832 | bytes 1835300 | tf_op jit(solution)/shard_map/dot_general | solution.py:47
  42.1 1.1 %fusion.7 = f32[53,1024]{1,0:T(8,128)S(1)} fusion(f32[53,1024]{1,0:T(8,128)S(1)} %fusion.9, f32[325,1024]{1,0:T(8,128)S(1)} %fusion.3, f32[53,1024]{1,0:T(8,128)S(1)} %bitcast.64, pred[1024]{0:T(1024)(128)(4,1)S(1)} %broadcast_bitcast_fusion, s32[325,53]{0,1:T(8,128)S(1)} %copy-done.3), kind=kOutput, calls=%fused_computation.19 | convolution fusion | flops 211949376 | bytes 2052388 | tf_op jit(solution)/shard_map/dot_general | solution.py:44
  43.2 1.5 %fusion.1 = f32[325,1024]{1,0:T(8,128)S(1)} fusion(f32[1024]{0:T(1024)S(1)} %bitcast_select_fusion, f32[325]{0:T(512)S(1)} %copy-done.5, f32[325]{0:T(512)S(1)} %copy-done.6, f32[53,1024]{1,0:T(8,128)S(1)} %fusion.7, s32[325,53]{0,1:T(8,128)S(1)} %copy-done.2), kind=kOutput, calls=%fused_computation.7 | convolution fusion | flops 212676416 | bytes 1623884 | tf_op jit(solution)/shard_map/dot_general | solution.py:39
  44.7 1.1 %fusion.15 = f32[53,1024]{1,0:T(8,128)S(1)} fusion(f32[53,1024]{1,0:T(8,128)S(1)} %fusion.7, f32[325,1024]{1,0:T(8,128)S(1)} %fusion.1, s32[325,53]{0,1:T(8,128)S(1)} %copy-done.2), kind=kOutput, calls=%fused_computation.27 | convolution fusion | flops 211786560 | bytes 1834276 | tf_op jit(solution)/shard_map/dot_general | solution.py:47
  45.8 1.1 %fusion.13 = f32[53,1024]{1,0:T(8,128)S(1)} fusion(f32[53,1024]{1,0:T(8,128)S(1)} %fusion.15, f32[53,1024]{1,0:T(8,128)S(1)} %fusion.7, f32[325,1024]{1,0:T(8,128)S(1)} %fusion.1, s32[325,53]{0,1:T(8,128)S(1)} %copy-done.3), kind=kOutput, calls=%fused_computation.25 | convolution fusion | flops 211895104 | bytes 2051364 | tf_op jit(solution)/shard_map/dot_general | solution.py:44
  47.0 0.8 %scatter_fusion = f32[53,16,128]{2,0,1:T(8,128)S(1)} fusion(f32[53,16,128]{2,0,1:T(8,128)S(1)} %bitcast.60, s32[8]{0:T(128)S(1)} %compare_select_fusion.2, f32[8,53,128]{2,1,0:T(8,128)S(1)} %bitcast.67), kind=kCustom, calls=%fused_computation.3 | custom fusion | bytes 651296 | tf_op jit(solution)/shard_map/scatter | solution.py:100
  47.8 0.8 %copy.28 = f32[53,2,8,128]{3,2,1,0:T(8,128)} copy(f32[53,2,8,128]{3,0,2,1:T(8,128)S(1)} %bitcast.61) | data formatting | bytes 868352 | tf_op jit(solution)/shard_map/reshape | solution.py:101
  (37 shorter events, 2.5 us)
Async XLA Ops:
  0.0 28.0 %copy-start = (f32[2,8,128]{2,1,0:T(8,128)S(1)}, f32[2,8,128]{2,1,0:T(8,128)}, u32[]{:S(2)}) copy-start(f32[2,8,128]{2,1,0:T(8,128)} %param.9) | copy-start | bytes 24580
  0.0 23.9 %copy-start.1 = (f32[53,2,8,128]{3,2,1,0:T(8,128)S(1)}, f32[53,2,8,128]{3,2,1,0:T(8,128)}, u32[]{:S(2)}) copy-start(f32[53,2,8,128]{3,2,1,0:T(8,128)} %param.8) | copy-start | bytes 1302532
  1.2 22.6 %collective-permute-start = (f32[53,2,8,128]{3,0,2,1:T(8,128)S(1)}, f32[53,2,8,128]{3,0,2,1:T(8,128)S(1)}, u32[]{:S(2)}, u32[]{:S(2)}) collective-permute-start(f32[53,2,8,128]{3,0,2,1:T(8,128)S(1)} %copy.21), channel_id=1, source_target_pairs={{0,4},{4,8},{8,12},{12,16},{16,20},{20,24},{24,28},{28,0},{1,5},{5... | collective-permute-start | bytes 1302536 | tf_op jit(solution)/shard_map/ppermute | solution.py:15
  4.3 21.8 %collective-permute-start.1 = (f32[53,2,8,128]{3,0,2,1:T(8,128)S(1)}, f32[53,2,8,128]{3,0,2,1:T(8,128)S(1)}, u32[]{:S(2)}, u32[]{:S(2)}) collective-permute-start(f32[53,2,8,128]{3,0,2,1:T(8,128)S(1)} %copy.21), channel_id=1, source_target_pairs={{4,0},{8,4},{12,8},{16,12},{20,16},{24,20},{28,24},{0,28},{5,1},{9... | collective-permute-start | bytes 1302536 | tf_op jit(solution)/shard_map/ppermute | solution.py:18
  26.2 8.6 %collective-permute-start.2 = (f32[53,6,2,128]{3,0,2,1:T(8,128)S(1)}, f32[53,6,2,128]{3,0,2,1:T(8,128)S(1)}, u32[]{:S(2)}, u32[]{:S(2)}) collective-permute-start(f32[53,6,2,128]{3,0,2,1:T(8,128)S(1)} %get-tuple-element.12), channel_id=1, source_target_pairs={{0,1},{1,2},{2,3},{3,0},{4,5},{5,6},{6,7},{7,4},{8,9},{9,10},{10,1... | collective-permute-start | bytes 976904 | tf_op jit(solution)/shard_map/ppermute | solution.py:15
  26.2 9.4 %collective-permute-start.3 = (f32[53,6,2,128]{3,0,2,1:T(8,128)S(1)}, f32[53,6,2,128]{3,0,2,1:T(8,128)S(1)}, u32[]{:S(2)}, u32[]{:S(2)}) collective-permute-start(f32[53,6,2,128]{3,0,2,1:T(8,128)S(1)} %get-tuple-element.11), channel_id=1, source_target_pairs={{1,0},{2,1},{3,2},{0,3},{5,4},{6,5},{7,6},{4,7},{9,8},{10,9},{11,1... | collective-permute-start | bytes 976904 | tf_op jit(solution)/shard_map/ppermute | solution.py:18
  36.1 0.7 %copy-start.4 = (f32[53]{0:T(128)S(1)}, f32[53]{0:T(128)}, u32[]{:S(2)}) copy-start(f32[53]{0:T(128)} %param.11) | copy-start | bytes 640
  38.7 0.9 %copy-start.2 = (s32[325,53]{0,1:T(8,128)S(1)}, s32[325,53]{0,1:T(8,128)}, u32[]{:S(2)}) copy-start(s32[325,53]{0,1:T(8,128)} %param.14) | copy-start | bytes 206704
  38.7 0.9 %copy-start.5 = (f32[325]{0:T(512)S(1)}, f32[325]{0:T(512)}, u32[]{:S(2)}) copy-start(f32[325]{0:T(512)} %param.13) | copy-start | bytes 3904
  38.7 0.9 %copy-start.6 = (f32[325]{0:T(512)S(1)}, f32[325]{0:T(512)}, u32[]{:S(2)}) copy-start(f32[325]{0:T(512)} %param.12) | copy-start | bytes 3904
  41.0 1.1 %copy-start.3 = (s32[325,53]{0,1:T(8,128)S(1)}, s32[325,53]{0,1:T(8,128)}, u32[]{:S(2)}) copy-start(s32[325,53]{0,1:T(8,128)} %param.15) | copy-start | bytes 206704
where the time goes:
time: 49.2 us; the launch traced here: 48.6 us
  waiting for transfers between devices  21.9 us (45%)
  starting transfers between devices  7.91 us (16%)
  local copies, waits for them, and re-layouts  7.43 us (15%)
  matrix products  7.22 us (15%)
  other arithmetic  3.88 us (8%)
    ppermute x2, waiting for transfers between devices, extended(): lax.ppermute(lax.slice_in_dim(block, block.shape[dim] - width, None, axis...  19 us
    ppermute x2, starting transfers between devices, extended(): lax.ppermute(lax.slice_in_dim(block, 0, width, axis=dim), axis, backward)  4.84 us
    ppermute x2, starting transfers between devices, extended(): lax.ppermute(lax.slice_in_dim(block, block.shape[dim] - width, None, axis...  3.08 us
    dot_general x2, matrix products, react(): jnp.dot(react_mat, logs, precision=lax.Precision.HIGHEST, preferred_eleme...  2.91 us
    ppermute x2, waiting for transfers between devices, extended(): lax.ppermute(lax.slice_in_dim(block, 0, width, axis=dim), axis, backward)  2.88 us
    dot_general x2, matrix products, react(): jnp.dot(prod_tr, rates, precision=lax.Precision.HIGHEST, preferred_elemen...  2.16 us
    dot_general x2, matrix products, react(): jnp.dot(react_tr, rates, precision=lax.Precision.HIGHEST, preferred_eleme...  2.14 us
    unnamed x20, local copies, waits for them, and re-layouts  1.96 us
  transfers between devices with their start and end apart: 4, of which 4 were waited for; matrix products, arithmetic and copies ran while one was open for 9% of the time, Pallas kernels for 0%

commit v1 on v0

v1 whole, which is shorter than its diff:
```python
import functools

import jax
import jax.numpy as jnp
from jax import lax
from jax.experimental import pallas as pl
from jax.experimental.pallas import tpu as pltpu
from jax.sharding import PartitionSpec as P

BURN_MAX = 8
CHUNKS = 4
MESH = pl.DeviceIdType.MESH


def pieces(total, count):
    edges = [total * i // count for i in range(count + 1)]
    return [(lo, hi - lo) for lo, hi in zip(edges[:-1], edges[1:])]


def in_plane(centre, up_edge, down_edge, row, coeff):
    last = centre.shape[1] - 1
    beside = jnp.where(row == 0, up_edge, pltpu.roll(centre, 1, 1))
    beside = beside + jnp.where(row == last, down_edge, pltpu.roll(centre, last, 1))
    beside = beside + pltpu.roll(centre, 1, 2) + pltpu.roll(centre, centre.shape[2] - 1, 2)
    return centre + coeff * (beside - 6.0 * centre)


def rolled(tile):
    return pltpu.roll(tile, 1, 1), pltpu.roll(tile, tile.shape[1] - 1, 1)


def exchange(
    n_wide, n_narrow, x_ref, c_ref, out_ref, xv, raw, corner_s, corner_r, halo_s, halo_r,
    sums_s, sums_r, local_sem, raw_ss, raw_rs, sums_ss, sums_rs, side_ss, side_rs,
):
    w, n = lax.axis_index("wide"), lax.axis_index("narrow")
    odd = w % 2
    near, far = 1 - odd, odd
    partner = w + 1 - 2 * odd
    target = (w + n_wide + 4 * odd - 2) % n_wide
    source = (w + n_wide + 2 - 4 * odd) % n_wide
    left, right = (n + n_narrow - 1) % n_narrow, (n + 1) % n_narrow
    nspec, _, cy, _ = xv.shape
    half = cy // 2
    chunks = pieces(nspec, CHUNKS)

    load = pltpu.make_async_copy(x_ref, xv, local_sem)
    load.start()
    barrier = pltpu.get_barrier_semaphore()
    for device in (
        (source, n), (source, left), (source, right), (w, left), (w, right), (partner, n)
    ):
        pl.semaphore_signal(barrier, inc=1, device_id=device, device_id_type=MESH)
    load.wait()
    corner_s[0] = xv[:, far, cy - 1, :]
    corner_s[1] = xv[:, far, 0, :]
    for start, size in chunks:
        sl = pl.ds(start, size)
        row = lax.broadcasted_iota(jnp.int32, (size,) + xv.shape[2:], 1)
        first, second = xv[sl, 0], pltpu.roll(xv[sl, 1], half, 1)
        halo_s[0, sl] = jnp.where(row >= half, first, second)
        halo_s[1, sl] = jnp.where(row < half, first, second)
    pl.semaphore_wait(barrier, 6)

    def send(src, dst, ss, rs, device):
        copy = pltpu.make_async_remote_copy(
            src_ref=src, dst_ref=dst, send_sem=ss, recv_sem=rs,
            device_id=device, device_id_type=MESH,
        )
        copy.start()
        return copy

    sides = [
        send(corner_s.at[0], corner_r.at[0], side_ss.at[0], side_rs.at[0], (target, right)),
        send(corner_s.at[1], corner_r.at[1], side_ss.at[1], side_rs.at[1], (target, left)),
        send(halo_s.at[0], halo_r.at[0], side_ss.at[2], side_rs.at[2], (w, right)),
        send(halo_s.at[1], halo_r.at[1], side_ss.at[3], side_rs.at[3], (w, left)),
    ]
    raws = []
    for k, (start, size) in enumerate(chunks):
        sl = pl.ds(start, size)
        raws.append(send(xv.at[sl], raw.at[sl], raw_ss.at[k], raw_rs.at[k], (target, n)))
    for copy in sides:
        copy.wait_recv()

    sums = []
    for k, (start, size) in enumerate(chunks):
        sl = pl.ds(start, size)
        coeff = c_ref[sl]
        square = coeff * coeff
        row = lax.broadcasted_iota(jnp.int32, (size,) + xv.shape[2:], 1)
        low, high = halo_r[0, sl], halo_r[1, sl]
        halos = (
            jnp.where(row < half, high, low),
            pltpu.roll(jnp.where(row < half, low, high), half, 1),
        )
        own_near, own_far = xv[sl, near], xv[sl, far]
        halo_near = jnp.where(near == 0, halos[0], halos[1])
        beyond = square * own_far + (2.0 * coeff) * in_plane(
            own_near, *rolled(halo_near), row, coeff
        )
        within = square * own_near
        raws[k].wait_recv()
        raw_near, raw_far = raw[sl, far], raw[sl, near]
        plane = in_plane(
            raw_near, corner_r[0, sl][:, None, :], corner_r[1, sl][:, None, :], row, coeff
        )
        sums_s[sl, near] = within + square * raw_far + (2.0 * coeff) * plane
        sums_s[sl, far] = beyond + square * raw_near
        sums.append(
            send(sums_s.at[sl], sums_r.at[sl], sums_ss.at[k], sums_rs.at[k], (partner, n))
        )
        for i in range(2):
            mine, other = xv[sl, i], xv[sl, 1 - i]
            centre = in_plane(mine, *rolled(halos[i]), row, coeff) + (2.0 * coeff) * other
            edge = in_plane(halos[i], *rolled(mine), row, coeff) + (2.0 * coeff) * halos[1 - i]
            out_ref[sl, i] = in_plane(centre, *rolled(edge), row, coeff) + (2.0 * square) * mine

    for k, (start, size) in enumerate(chunks):
        sl = pl.ds(start, size)
        sums[k].wait_recv()
        out_ref[sl] = out_ref[sl] + sums_r[sl]
    for copy in sides + raws + sums:
        copy.wait_send()


def two_parts(values):
    high = values.astype(jnp.bfloat16)
    return high, (values - high.astype(jnp.float32)).astype(jnp.bfloat16)


def reaction(
    marks_ref, mixed_ref, heat_ref, scale_ref, energy_ref, logs_ref, sums_ref, out_ref,
    picked, temps, stacked, slots,
):
    nspec = mixed_ref.shape[0] // heat_ref.shape[0]
    stacks, height = heat_ref.shape
    per_row = marks_ref.shape[1]
    room = stacked.shape[0] // 2
    pad = sums_ref.shape[0] // 2
    out_ref[...] = mixed_ref[...]
    for k in range(BURN_MAX):
        slots[k] = 0
    count = jnp.int32(0)
    for i in range(stacks):
        burning = marks_ref[i // per_row, i % per_row]

        @pl.when((burning == 1) & (count < BURN_MAX))
        def _():
            slots[count] = i

        count = count + burning
    for k in range(BURN_MAX):
        cells = pl.ds(k * height, height)
        picked[:, cells] = mixed_ref[pl.ds(slots[k], nspec, stride=stacks), :]
        temps[:, cells] = heat_ref[pl.ds(slots[k], 1), :]
    stacked[...] = jnp.zeros_like(stacked)
    base = scale_ref[...] - energy_ref[...] * (1.0 / temps[...])
    values = picked[...]
    for substep in range(2):
        high, low = two_parts(jnp.log(values))
        stacked[0:nspec, :] = high
        stacked[room : room + nspec, :] = low
        expo = base + jnp.dot(logs_ref[...], stacked[...], preferred_element_type=jnp.float32)
        high, low = two_parts(jnp.exp(expo))
        total = jnp.dot(sums_ref[...], high, preferred_element_type=jnp.float32)
        total = total + jnp.dot(sums_ref[...], low, preferred_element_type=jnp.float32)
        gain, loss = total[0:nspec], total[pad : pad + nspec]
        values = values * (values + 0.5 * gain) / (values + 0.5 * loss)
    picked[...] = values
    for k in range(BURN_MAX):

        @pl.when(k < count)
        def _():
            column = picked[:, k * height : (k + 1) * height]
            out_ref[pl.ds(slots[k], nspec, stride=stacks), :] = column


def round_up(value, step):
    return -(-value // step) * step


def shards(
    n_wide,
    n_narrow,
    chemical_fractions,
    thermal_state,
    ignited_stacks,
    spreading_number,
    natural_exponent_scale,
    arrhenius_energy,
    incoming_stoichiometry,
    outgoing_stoichiometry,
):
    shape = chemical_fractions.shape
    nspec, cx, cy, height = shape
    nreact = incoming_stoichiometry.shape[0]
    f32, bf16 = jnp.float32, jnp.bfloat16
    vmem = pl.BlockSpec(memory_space=pltpu.VMEM)
    smem = pl.BlockSpec(memory_space=pltpu.SMEM)
    coeff = jnp.broadcast_to(spreading_number[:, None, None], (nspec, 1, height))
    dma = pltpu.SemaphoreType.DMA
    mixed = pl.pallas_call(
        functools.partial(exchange, n_wide, n_narrow),
        out_shape=jax.ShapeDtypeStruct(shape, f32),
        in_specs=[pl.BlockSpec(memory_space=pl.ANY), vmem],
        out_specs=vmem,
        scratch_shapes=[
            pltpu.VMEM(shape, f32),
            pltpu.VMEM(shape, f32),
            pltpu.VMEM((2, nspec, height), f32),
            pltpu.VMEM((2, nspec, height), f32),
            pltpu.VMEM((2, nspec, cy, height), f32),
            pltpu.VMEM((2, nspec, cy, height), f32),
            pltpu.VMEM(shape, f32),
            pltpu.VMEM(shape, f32),
            dma(()),
            dma((CHUNKS,)),
            dma((CHUNKS,)),
            dma((CHUNKS,)),
            dma((CHUNKS,)),
            dma((4,)),
            dma((4,)),
        ],
        compiler_params=pltpu.CompilerParams(
            collective_id=0, has_side_effects=True, vmem_limit_bytes=32 * 2**20
        ),
        name="exchange",
    )(chemical_fractions, coeff)

    room, rows = round_up(nspec, 64), round_up(nreact, 16)
    pad = round_up(nspec, 8)
    more = rows - nreact
    incoming = jnp.pad(incoming_stoichiometry.astype(bf16), ((0, more), (0, 0)))
    outgoing = jnp.pad(outgoing_stoichiometry.astype(bf16), ((0, more), (0, 0)))
    logs_mat = jnp.tile(jnp.pad(incoming, ((0, 0), (0, room - nspec))), (1, 2))
    sums_mat = jnp.concatenate(
        [jnp.pad(m, ((0, 0), (0, pad - nspec))) for m in (outgoing, incoming)], axis=1
    ).T
    cells = BURN_MAX * height
    updated = pl.pallas_call(
        reaction,
        out_shape=jax.ShapeDtypeStruct((nspec * cx * cy, height), f32),
        in_specs=[smem] + [vmem] * 6,
        out_specs=vmem,
        scratch_shapes=[
            pltpu.VMEM((nspec, cells), f32),
            pltpu.VMEM((1, cells), f32),
            pltpu.VMEM((2 * room, cells), bf16),
            pltpu.SMEM((BURN_MAX,), jnp.int32),
        ],
        compiler_params=pltpu.CompilerParams(vmem_limit_bytes=32 * 2**20),
        name="reaction",
    )(
        ignited_stacks,
        mixed.reshape(nspec * cx * cy, height),
        thermal_state.reshape(cx * cy, height),
        jnp.pad(natural_exponent_scale, (0, more))[:, None],
        jnp.pad(arrhenius_energy, (0, more))[:, None],
        logs_mat,
        sums_mat,
    )
    return updated.reshape(shape)


def solution(mesh):
    in_specs = (
        P(None, "wide", "narrow", None),
        P("wide", "narrow", None),
        P("wide", "narrow"),
        P(),
        P(),
        P(),
        P(),
        P(),
    )
    out_specs = P(None, "wide", "narrow", None)
    body = functools.partial(shards, mesh.shape["wide"], mesh.shape["narrow"])
    return jax.shard_map(body, mesh=mesh, in_specs=in_specs, out_specs=out_specs, check_vma=False)
```

time: 49.2 us -> 31 us (0.63)
  Pallas kernels: 0 us -> 26.6 us
  waiting for transfers between devices: 21.9 us -> 0 us
  starting transfers between devices: 7.91 us -> 0 us
  matrix products: 7.22 us -> 0 us
  local copies, waits for them, and re-layouts: 7.43 us -> 3.1 us
  other arithmetic: 3.88 us -> 0.95 us
    pallas_call x0 -> x2, Pallas kernels: none -> 26.6 us  [the longest x1 23.5 us: shards(): pl.pallas_call(functools.partial(exchange, n_wide, n_narrow), out_shape=j...]
    ppermute x4 -> x0, waiting for transfers between devices: 21.9 us -> none  [the longest x2 19 us: extended(): lax.ppermute(lax.slice_in_dim(block, block.shape[dim] - width, None, axis...]
    ppermute x4 -> x0, starting transfers between devices: 7.91 us -> none  [the longest x2 4.84 us: extended(): lax.ppermute(lax.slice_in_dim(block, 0, width, axis=dim), axis, backward)]
    dot_general x6 -> x0, matrix products: 7.22 us -> none  [the longest x2 2.91 us: react(): jnp.dot(react_mat, logs, precision=lax.Precision.HIGHEST, preferred_eleme...]
    reshape x4 -> x0, local copies, waits for them, and re-layouts: 1.66 us -> none  [the longest x1 0.84 us: shards(): return flat.reshape(nspec, cols_x, cols_y, mesh_volumes)]
    add x2 -> x0, other arithmetic: 1.53 us -> none  [diffuse_padded(): return centre + coeff * (beside - 6.0 * centre)]
    scatter x2 -> x0, local copies, waits for them, and re-layouts: 1.39 us -> none  [the longest x1 0.77 us: shards(): flat = flat.at[:, spot].set(result, mode='drop')]
    reduce_sum x1 -> x0, other arithmetic: 1.32 us -> none  [shards(): count = jnp.sum(marks)]
  transfers between devices with their start and end apart: 4 -> 0, of which waited for: 4 -> 0; matrix products, arithmetic and copies ran while one was open for 9% -> 0% of each run, Pallas kernels for 0% -> 0%
where the time goes in v1:
time: 31 us; the launch traced here: 30.8 us
  Pallas kernels  26.6 us (86%)
  local copies, waits for them, and re-layouts  3.1 us (10%)
  other arithmetic  0.95 us (3%)
    pallas_call x1, Pallas kernels, shards(): pl.pallas_call(functools.partial(exchange, n_wide, n_narrow), out_shape=j...  23.5 us
    pallas_call x1, Pallas kernels, shards(): pl.pallas_call(reaction, out_shape=jax.ShapeDtypeStruct((nspec * cx * cy,...  3.15 us
    unnamed x12, local copies, waits for them, and re-layouts  1.92 us
    convert_element_type x1, other arithmetic, shards(): incoming = jnp.pad(incoming_stoichiometry.astype(bf16), ((0, more), (0, 0)))  0.93 us
    pad x1, local copies, waits for them, and re-layouts, shards(): jnp.pad(natural_exponent_scale, (0, more))[:, None]  0.7 us

profile of v1, /device:TPU:0, one launch (start us, length us, event | category | flops | bytes accessed | tf_op | source)
XLA Modules:
  0.0 30.8 jit_solution(619952590967479340)
XLA Ops:
  0.0 0.0 copy-start.4
  0.0 0.7 %pad.25 = f32[336]{0:T(512)S(1)} pad(f32[325]{0:T(512)} %param.12, f32[]{:T(128)} %constant.3.clone.1), padding=0_11 | pad | bytes 2648 | tf_op jit(solution)/shard_map/jit(_pad)/pad | solution.py:258
  0.7 0.0 copy-done.4
  0.7 0.0 copy-start.5
  0.7 0.6 %copy-done.5 = f32[53]{0:T(128)S(1)} copy-done((f32[53]{0:T(128)S(1)}, f32[53]{0:T(128)}, u32[]{:S(2)}) %copy-start.5) | copy-done | bytes 236
  1.4 0.1 broadcast_in_dim.12.c_ref
  1.5 0.0 copy-start.3
  1.5 0.9 %convert_element_type.17 = bf16[325,53]{0,1:T(8,128)(2,1)S(1)} convert(s32[325,53]{0,1:T(8,128)} %param.14) | non-fusion elementwise | flops 17225 | bytes 103350 | tf_op jit(solution)/shard_map/convert_element_type | solution.py:234
  2.4 0.0 copy-done.3
  2.5 0.0 copy-start
  2.5 0.1 copy.12.logs_ref
  2.7 0.1 broadcast_in_dim.16.energy_ref
  2.8 0.1 broadcast_in_dim.15.scale_ref
  2.9 0.6 %copy-done = f32[53,2,8,128]{3,2,1,0:T(8,128)S(1)} copy-done((f32[53,2,8,128]{3,2,1,0:T(8,128)S(1)}, f32[53,2,8,128]{3,2,1,0:T(8,128)}, u32[]{:S(2)}) %copy-start) | copy-done | bytes 434200
  3.5 0.0 copy-start.1
  3.5 23.5 %exchange.1 = f32[53,2,8,128]{3,2,1,0:T(8,128)S(1)} custom-call(f32[53,2,8,128]{3,2,1,0:T(8,128)S(1)} %copy-done, f32[53,1,128]{2,1,0:T(1,128)S(1)} %broadcast_in_dim.12.c_ref), custom_call_target="tpu_custom_call" | custom-call | tf_op jit(solution)/shard_map/exchange/pallas_call | solution.py:203
  27.0 0.0 copy-start.2
  27.0 0.0 copy-done.1
  27.0 0.7 %copy-done.2 = s32[2,8]{1,0:T(2,128)S(1)} copy-done((s32[2,8]{1,0:T(2,128)S(1)}, s32[2,8]{1,0:T(2,128)}, u32[]{:S(2)}) %copy-start.2) | copy-done | bytes 88
  27.7 3.1 %reaction.1 = f32[848,128]{1,0:T(8,128)} custom-call(s32[2,8]{1,0:T(2,128)S(1)} %copy-done.2, f32[848,128]{1,0:T(8,128)S(1)} %bitcast.6, f32[16,128]{1,0:T(8,128)S(1)} %bitcast.7, f32[336,1]{1,0:T(8,128)S(1)} %broadcast_in_dim.15.scale_ref, f32[336,1]{1,0:T(8,128)S(1)} %broadcast_in_dim.16.energy_ref, bf16[336,128]{1,0:T(8,128)(2,1)S(1)} %copy.12.logs_ref, ...), custom_call_target="tpu_custom_call" | custom-call | tf_op jit(solution)/shard_map/reaction/pallas_call | solution.py:241
  (6 shorter events, 0.1 us)
Async XLA Ops:
  0.0 0.7 %copy-start.4 = (f32[325]{0:T(512)S(1)}, f32[325]{0:T(512)}, u32[]{:S(2)}) copy-start(f32[325]{0:T(512)} %param.13) | copy-start | bytes 3904
  0.7 0.7 %copy-start.5 = (f32[53]{0:T(128)S(1)}, f32[53]{0:T(128)}, u32[]{:S(2)}) copy-start(f32[53]{0:T(128)} %param.11) | copy-start | bytes 640
  1.5 1.0 %copy-start.3 = (s32[325,53]{0,1:T(8,128)S(1)}, s32[325,53]{0,1:T(8,128)}, u32[]{:S(2)}) copy-start(s32[325,53]{0,1:T(8,128)} %param.15) | copy-start | bytes 206704
  2.5 1.0 %copy-start = (f32[53,2,8,128]{3,2,1,0:T(8,128)S(1)}, f32[53,2,8,128]{3,2,1,0:T(8,128)}, u32[]{:S(2)}) copy-start(f32[53,2,8,128]{3,2,1,0:T(8,128)} %x_ref.1) | copy-start | bytes 1302532
  3.5 23.5 %copy-start.1 = (f32[2,8,128]{2,1,0:T(8,128)S(1)}, f32[2,8,128]{2,1,0:T(8,128)}, u32[]{:S(2)}) copy-start(f32[2,8,128]{2,1,0:T(8,128)} %param.9) | copy-start | bytes 24580
  27.0 0.7 %copy-start.2 = (s32[2,8]{1,0:T(2,128)S(1)}, s32[2,8]{1,0:T(2,128)}, u32[]{:S(2)}) copy-start(s32[2,8]{1,0:T(2,128)} %marks_ref.1) | copy-start | bytes 196

commit v2 on v1

--- a/solution.py
+++ b/solution.py
@@ -8,7 +8,7 @@
 from jax.sharding import PartitionSpec as P
 
 BURN_MAX = 8
-CHUNKS = 4
+CHUNKS = 8
 MESH = pl.DeviceIdType.MESH
 
 
@@ -30,8 +30,9 @@
 
 
 def exchange(
-    n_wide, n_narrow, x_ref, c_ref, out_ref, xv, raw, corner_s, corner_r, halo_s, halo_r,
-    sums_s, sums_r, local_sem, raw_ss, raw_rs, sums_ss, sums_rs, side_ss, side_rs,
+    n_wide, n_narrow, x_ref, c_ref, out_ref, xv, raw, corner_s, corner_r, edge_s, edge_r,
+    rest_s, rest_r, sums_s, sums_r, local_sem, raw_ss, raw_rs, sums_ss, sums_rs,
+    side_ss, side_rs,
 ):
     w, n = lax.axis_index("wide"), lax.axis_index("narrow")
     odd = w % 2
@@ -41,7 +42,6 @@
     source = (w + n_wide + 2 - 4 * odd) % n_wide
     left, right = (n + n_narrow - 1) % n_narrow, (n + 1) % n_narrow
     nspec, _, cy, _ = xv.shape
-    half = cy // 2
     chunks = pieces(nspec, CHUNKS)
 
     load = pltpu.make_async_copy(x_ref, xv, local_sem)
@@ -52,14 +52,12 @@
     ):
         pl.semaphore_signal(barrier, inc=1, device_id=device, device_id_type=MESH)
     load.wait()
-    corner_s[0] = xv[:, far, cy - 1, :]
-    corner_s[1] = xv[:, far, 0, :]
-    for start, size in chunks:
-        sl = pl.ds(start, size)
-        row = lax.broadcasted_iota(jnp.int32, (size,) + xv.shape[2:], 1)
-        first, second = xv[sl, 0], pltpu.roll(xv[sl, 1], half, 1)
-        halo_s[0, sl] = jnp.where(row >= half, first, second)
-        halo_s[1, sl] = jnp.where(row < half, first, second)
+    for side, (row, inner) in enumerate(((cy - 1, cy - 2), (0, 1))):
+        corner_s[side] = xv[:, far, row, :]
+        edge_s[side] = xv[:, near, row, :]
+        rest_s[side, 0] = xv[:, far, row, :]
+        rest_s[side, 1] = xv[:, near, inner, :]
+        rest_s[side, 2] = xv[:, far, inner, :]
     pl.semaphore_wait(barrier, 6)
 
     def send(src, dst, ss, rs, device):
@@ -70,57 +68,79 @@
         copy.start()
         return copy
 
-    sides = [
-        send(corner_s.at[0], corner_r.at[0], side_ss.at[0], side_rs.at[0], (target, right)),
-        send(corner_s.at[1], corner_r.at[1], side_ss.at[1], side_rs.at[1], (target, left)),
-        send(halo_s.at[0], halo_r.at[0], side_ss.at[2], side_rs.at[2], (w, right)),
-        send(halo_s.at[1], halo_r.at[1], side_ss.at[3], side_rs.at[3], (w, left)),
+    raws, sums = [], []
+
+    def send_raw(k):
+        sl = pl.ds(*chunks[k])
+        raws.append(send(xv.at[sl], raw.at[sl], raw_ss.at[k], raw_rs.at[k], (target, n)))
+
+    send_raw(0)
+    sides = []
+    for side, to in enumerate((right, left)):
+        for j, (src, dst, device) in enumerate((
+            (corner_s, corner_r, (target, to)),
+            (edge_s, edge_r, (w, to)),
+        )):
+            at = 2 * j + side
+            sides.append(
+                send(src.at[side], dst.at[side], side_ss.at[at], side_rs.at[at], device)
+            )
+    send_raw(1)
+    rests = [
+        send(rest_s.at[side], rest_r.at[side], side_ss.at[4 + side], side_rs.at[4 + side], (w, to))
+        for side, to in enumerate((right, left))
     ]
-    raws = []
-    for k, (start, size) in enumerate(chunks):
-        sl = pl.ds(start, size)
-        raws.append(send(xv.at[sl], raw.at[sl], raw_ss.at[k], raw_rs.at[k], (target, n)))
     for copy in sides:
         copy.wait_recv()
 
-    sums = []
     for k, (start, size) in enumerate(chunks):
         sl = pl.ds(start, size)
         coeff = c_ref[sl]
-        square = coeff * coeff
+        square, twice = coeff * coeff, 2.0 * coeff
         row = lax.broadcasted_iota(jnp.int32, (size,) + xv.shape[2:], 1)
-        low, high = halo_r[0, sl], halo_r[1, sl]
-        halos = (
-            jnp.where(row < half, high, low),
-            pltpu.roll(jnp.where(row < half, low, high), half, 1),
-        )
+        low, high = edge_r[0, sl][:, None, :], edge_r[1, sl][:, None, :]
         own_near, own_far = xv[sl, near], xv[sl, far]
-        halo_near = jnp.where(near == 0, halos[0], halos[1])
-        beyond = square * own_far + (2.0 * coeff) * in_plane(
-            own_near, *rolled(halo_near), row, coeff
-        )
-        within = square * own_near
+        plane = in_plane(own_near, low, high, row, coeff)
         raws[k].wait_recv()
+        if k + 2 < len(chunks):
+            send_raw(k + 2)
         raw_near, raw_far = raw[sl, far], raw[sl, near]
-        plane = in_plane(
+        sums_s[sl, far] = twice * plane + square * (own_far + raw_near)
+        beyond = in_plane(
             raw_near, corner_r[0, sl][:, None, :], corner_r[1, sl][:, None, :], row, coeff
         )
-        sums_s[sl, near] = within + square * raw_far + (2.0 * coeff) * plane
-        sums_s[sl, far] = beyond + square * raw_near
+        sums_s[sl, near] = twice * beyond + square * (own_near + raw_far)
         sums.append(
             send(sums_s.at[sl], sums_r.at[sl], sums_ss.at[k], sums_rs.at[k], (partner, n))
         )
-        for i in range(2):
-            mine, other = xv[sl, i], xv[sl, 1 - i]
-            centre = in_plane(mine, *rolled(halos[i]), row, coeff) + (2.0 * coeff) * other
-            edge = in_plane(halos[i], *rolled(mine), row, coeff) + (2.0 * coeff) * halos[1 - i]
-            out_ref[sl, i] = in_plane(centre, *rolled(edge), row, coeff) + (2.0 * square) * mine
+        if k == 0:
+            for copy in rests:
+                copy.wait_recv()
+
+        def halo(low, high, low_inner, high_inner):
+            tile = jnp.where(row == 0, high, high_inner[:, None, :])
+            return jnp.where(row == cy - 1, low, jnp.where(row == cy - 2, low_inner[:, None, :], tile))
+
+        halo_near = halo(low, high, rest_r[0, 1, sl], rest_r[1, 1, sl])
+        halo_far = halo(
+            rest_r[0, 0, sl][:, None, :], rest_r[1, 0, sl][:, None, :],
+            rest_r[0, 2, sl], rest_r[1, 2, sl],
+        )
+        for at, mine, other, side, across, flat in (
+            (near, own_near, own_far, halo_near, halo_far, plane),
+            (far, own_far, own_near, halo_far, halo_near, None),
+        ):
+            if flat is None:
+                flat = in_plane(mine, *rolled(side), row, coeff)
+            centre = flat + twice * other
+            edge = in_plane(side, *rolled(mine), row, coeff) + twice * across
+            out_ref[sl, at] = in_plane(centre, *rolled(edge), row, coeff) + 2.0 * square * mine
 
     for k, (start, size) in enumerate(chunks):
         sl = pl.ds(start, size)
         sums[k].wait_recv()
         out_ref[sl] = out_ref[sl] + sums_r[sl]
-    for copy in sides + raws + sums:
+    for copy in sides + rests + raws + sums:
         copy.wait_send()
 
 
@@ -210,8 +230,10 @@
             pltpu.VMEM(shape, f32),
             pltpu.VMEM((2, nspec, height), f32),
             pltpu.VMEM((2, nspec, height), f32),
-            pltpu.VMEM((2, nspec, cy, height), f32),
-            pltpu.VMEM((2, nspec, cy, height), f32),
+            pltpu.VMEM((2, nspec, height), f32),
+            pltpu.VMEM((2, nspec, height), f32),
+            pltpu.VMEM((2, 3, nspec, height), f32),
+            pltpu.VMEM((2, 3, nspec, height), f32),
             pltpu.VMEM(shape, f32),
             pltpu.VMEM(shape, f32),
             dma(()),
@@ -219,8 +241,8 @@
             dma((CHUNKS,)),
             dma((CHUNKS,)),
             dma((CHUNKS,)),
-            dma((4,)),
-            dma((4,)),
+            dma((6,)),
+            dma((6,)),
         ],
         compiler_params=pltpu.CompilerParams(
             collective_id=0, has_side_effects=True, vmem_limit_bytes=32 * 2**20

time: 31 us -> 32.8 us (1.058)
  Pallas kernels: 26.6 us -> 28.3 us
    pallas_call x1, Pallas kernels: 23.5 us -> 25.2 us  [shards(): pl.pallas_call(functools.partial(exchange, n_wide, n_narrow), out_shape=j...]
where the time goes in v2:
time: 32.8 us; the launch traced here: 32.5 us
  Pallas kernels  28.3 us (86%)
  local copies, waits for them, and re-layouts  3.1 us (9%)
  other arithmetic  0.95 us (3%)
    pallas_call x1, Pallas kernels, shards(): pl.pallas_call(functools.partial(exchange, n_wide, n_narrow), out_shape=j...  25.2 us
    pallas_call x1, Pallas kernels, shards(): pl.pallas_call(reaction, out_shape=jax.ShapeDtypeStruct((nspec * cx * cy,...  3.08 us
    unnamed x12, local copies, waits for them, and re-layouts  1.92 us
    convert_element_type x1, other arithmetic, shards(): incoming = jnp.pad(incoming_stoichiometry.astype(bf16), ((0, more), (0, 0)))  0.93 us
    pad x1, local copies, waits for them, and re-layouts, shards(): jnp.pad(natural_exponent_scale, (0, more))[:, None]  0.7 us

profile of v2, /device:TPU:0, one launch (start us, length us, event | category | flops | bytes accessed | tf_op | source)
XLA Modules:
  0.0 32.5 jit_solution(17600928142370220297)
XLA Ops:
  0.0 0.0 copy-start.4
  0.0 0.7 %pad.25 = f32[336]{0:T(512)S(1)} pad(f32[325]{0:T(512)} %param.12, f32[]{:T(128)} %constant.3.clone.1), padding=0_11 | pad | bytes 2648 | tf_op jit(solution)/shard_map/jit(_pad)/pad | solution.py:280
  0.7 0.0 copy-done.4
  0.7 0.0 copy-start.5
  0.7 0.6 %copy-done.5 = f32[53]{0:T(128)S(1)} copy-done((f32[53]{0:T(128)S(1)}, f32[53]{0:T(128)}, u32[]{:S(2)}) %copy-start.5) | copy-done | bytes 236
  1.4 0.1 broadcast_in_dim.12.c_ref
  1.5 0.0 copy-start.3
  1.5 0.9 %convert_element_type.17 = bf16[325,53]{0,1:T(8,128)(2,1)S(1)} convert(s32[325,53]{0,1:T(8,128)} %param.14) | non-fusion elementwise | flops 17225 | bytes 103350 | tf_op jit(solution)/shard_map/convert_element_type | solution.py:256
  2.4 0.0 copy-done.3
  2.5 0.0 copy-start
  2.5 0.1 copy.12.logs_ref
  2.7 0.1 broadcast_in_dim.16.energy_ref
  2.8 0.1 broadcast_in_dim.15.scale_ref
  2.9 0.6 %copy-done = f32[53,2,8,128]{3,2,1,0:T(8,128)S(1)} copy-done((f32[53,2,8,128]{3,2,1,0:T(8,128)S(1)}, f32[53,2,8,128]{3,2,1,0:T(8,128)}, u32[]{:S(2)}) %copy-start) | copy-done | bytes 434200
  3.5 0.0 copy-start.1
  3.5 25.2 %exchange.1 = f32[53,2,8,128]{3,2,1,0:T(8,128)S(1)} custom-call(f32[53,2,8,128]{3,2,1,0:T(8,128)S(1)} %copy-done, f32[53,1,128]{2,1,0:T(1,128)S(1)} %broadcast_in_dim.12.c_ref), custom_call_target="tpu_custom_call" | custom-call | tf_op jit(solution)/shard_map/exchange/pallas_call | solution.py:223
  28.7 0.0 copy-start.2
  28.7 0.0 copy-done.1
  28.7 0.7 %copy-done.2 = s32[2,8]{1,0:T(2,128)S(1)} copy-done((s32[2,8]{1,0:T(2,128)S(1)}, s32[2,8]{1,0:T(2,128)}, u32[]{:S(2)}) %copy-start.2) | copy-done | bytes 88
  29.4 3.1 %reaction.1 = f32[848,128]{1,0:T(8,128)} custom-call(s32[2,8]{1,0:T(2,128)S(1)} %copy-done.2, f32[848,128]{1,0:T(8,128)S(1)} %bitcast.6, f32[16,128]{1,0:T(8,128)S(1)} %bitcast.7, f32[336,1]{1,0:T(8,128)S(1)} %broadcast_in_dim.15.scale_ref, f32[336,1]{1,0:T(8,128)S(1)} %broadcast_in_dim.16.energy_ref, bf16[336,128]{1,0:T(8,128)(2,1)S(1)} %copy.12.logs_ref, ...), custom_call_target="tpu_custom_call" | custom-call | tf_op jit(solution)/shard_map/reaction/pallas_call | solution.py:263
  (6 shorter events, 0.1 us)
Async XLA Ops:
  0.0 0.7 %copy-start.4 = (f32[325]{0:T(512)S(1)}, f32[325]{0:T(512)}, u32[]{:S(2)}) copy-start(f32[325]{0:T(512)} %param.13) | copy-start | bytes 3904
  0.7 0.7 %copy-start.5 = (f32[53]{0:T(128)S(1)}, f32[53]{0:T(128)}, u32[]{:S(2)}) copy-start(f32[53]{0:T(128)} %param.11) | copy-start | bytes 640
  1.5 1.0 %copy-start.3 = (s32[325,53]{0,1:T(8,128)S(1)}, s32[325,53]{0,1:T(8,128)}, u32[]{:S(2)}) copy-start(s32[325,53]{0,1:T(8,128)} %param.15) | copy-start | bytes 206704
  2.5 1.0 %copy-start = (f32[53,2,8,128]{3,2,1,0:T(8,128)S(1)}, f32[53,2,8,128]{3,2,1,0:T(8,128)}, u32[]{:S(2)}) copy-start(f32[53,2,8,128]{3,2,1,0:T(8,128)} %x_ref.1) | copy-start | bytes 1302532
  3.5 25.3 %copy-start.1 = (f32[2,8,128]{2,1,0:T(8,128)S(1)}, f32[2,8,128]{2,1,0:T(8,128)}, u32[]{:S(2)}) copy-start(f32[2,8,128]{2,1,0:T(8,128)} %param.9) | copy-start | bytes 24580
  28.7 0.7 %copy-start.2 = (s32[2,8]{1,0:T(2,128)S(1)}, s32[2,8]{1,0:T(2,128)}, u32[]{:S(2)}) copy-start(s32[2,8]{1,0:T(2,128)} %marks_ref.1) | copy-start | bytes 196

commit v3 on v1

--- a/solution.py
+++ b/solution.py
@@ -8,7 +8,8 @@
 from jax.sharding import PartitionSpec as P
 
 BURN_MAX = 8
-CHUNKS = 4
+EARLY = 3
+LATE = 3
 MESH = pl.DeviceIdType.MESH
 
 
@@ -30,37 +31,40 @@
 
 
 def exchange(
-    n_wide, n_narrow, x_ref, c_ref, out_ref, xv, raw, corner_s, corner_r, halo_s, halo_r,
-    sums_s, sums_r, local_sem, raw_ss, raw_rs, sums_ss, sums_rs, side_ss, side_rs,
+    n_wide, n_narrow, x_ref, c_ref, out_ref, xv, raw, sums_s, sums_r, part, beyond,
+    corner_s, corner_r, touch_s, touch_r, edge_s, edge_r, rest_s, rest_r, local_sem,
+    raw_ss, raw_rs, sums_ss, sums_rs, part_ss, part_rs, pass_ss, pass_rs, side_ss, side_rs,
 ):
     w, n = lax.axis_index("wide"), lax.axis_index("narrow")
     odd = w % 2
     near, far = 1 - odd, odd
     partner = w + 1 - 2 * odd
+    other = (w + n_wide + 2 * odd - 1) % n_wide
     target = (w + n_wide + 4 * odd - 2) % n_wide
     source = (w + n_wide + 2 - 4 * odd) % n_wide
     left, right = (n + n_narrow - 1) % n_narrow, (n + 1) % n_narrow
     nspec, _, cy, _ = xv.shape
-    half = cy // 2
-    chunks = pieces(nspec, CHUNKS)
+    early, late = raw.shape[0], part.shape[0]
+    early_chunks, late_chunks = pieces(early, EARLY), pieces(late, LATE)
 
     load = pltpu.make_async_copy(x_ref, xv, local_sem)
     load.start()
     barrier = pltpu.get_barrier_semaphore()
-    for device in (
-        (source, n), (source, left), (source, right), (w, left), (w, right), (partner, n)
-    ):
+    greeted = [(w, left), (w, right)]
+    greeted += [(a, b) for a in (source, partner) for b in (n, left, right)]
+    greeted += [(other, left), (other, right), (target, n)]
+    for device in greeted:
         pl.semaphore_signal(barrier, inc=1, device_id=device, device_id_type=MESH)
     load.wait()
-    corner_s[0] = xv[:, far, cy - 1, :]
-    corner_s[1] = xv[:, far, 0, :]
-    for start, size in chunks:
-        sl = pl.ds(start, size)
-        row = lax.broadcasted_iota(jnp.int32, (size,) + xv.shape[2:], 1)
-        first, second = xv[sl, 0], pltpu.roll(xv[sl, 1], half, 1)
-        halo_s[0, sl] = jnp.where(row >= half, first, second)
-        halo_s[1, sl] = jnp.where(row < half, first, second)
-    pl.semaphore_wait(barrier, 6)
+    for side, (row, inner) in enumerate(((cy - 1, cy - 2), (0, 1))):
+        corner_s[side] = xv[0:early, far, row, :]
+        touch_s[side, 0] = xv[early:nspec, near, row, :]
+        touch_s[side, 1] = xv[early:nspec, far, row, :]
+        edge_s[side] = xv[:, near, row, :]
+        rest_s[side, 0] = xv[:, far, row, :]
+        rest_s[side, 1] = xv[:, near, inner, :]
+        rest_s[side, 2] = xv[:, far, inner, :]
+    pl.semaphore_wait(barrier, len(greeted))
 
     def send(src, dst, ss, rs, device):
         copy = pltpu.make_async_remote_copy(
@@ -70,57 +74,113 @@
         copy.start()
         return copy
 
-    sides = [
-        send(corner_s.at[0], corner_r.at[0], side_ss.at[0], side_rs.at[0], (target, right)),
-        send(corner_s.at[1], corner_r.at[1], side_ss.at[1], side_rs.at[1], (target, left)),
-        send(halo_s.at[0], halo_r.at[0], side_ss.at[2], side_rs.at[2], (w, right)),
-        send(halo_s.at[1], halo_r.at[1], side_ss.at[3], side_rs.at[3], (w, left)),
-    ]
-    raws = []
-    for k, (start, size) in enumerate(chunks):
-        sl = pl.ds(start, size)
-        raws.append(send(xv.at[sl], raw.at[sl], raw_ss.at[k], raw_rs.at[k], (target, n)))
-    for copy in sides:
+    def sides_of(at, src, dst, row):
+        return [
+            send(src(side), dst(side), side_ss.at[at + side], side_rs.at[at + side], (row, to))
+            for side, to in enumerate((right, left))
+        ]
+
+    corners = sides_of(0, lambda i: corner_s.at[i], lambda i: corner_r.at[i], target)
+    edges = sides_of(2, lambda i: edge_s.at[i], lambda i: edge_r.at[i], w)
+    raws, parts = [], []
+    for k in range(max(EARLY, LATE)):
+        if k < EARLY:
+            sl = pl.ds(*early_chunks[k])
+            raws.append(send(xv.at[sl], raw.at[sl], raw_ss.at[k], raw_rs.at[k], (target, n)))
+        if k < LATE:
+            start, size = late_chunks[k]
+            parts.append(
+                send(
+                    xv.at[pl.ds(early + start, size)], part.at[pl.ds(start, size)],
+                    part_ss.at[k], part_rs.at[k], (partner, n),
+                )
+            )
+    rests = sides_of(4, lambda i: rest_s.at[i], lambda i: rest_r.at[i], w)
+    touches = sides_of(6, lambda i: touch_s.at[i, 0], lambda i: touch_r.at[i, 0], partner)
+    touches += sides_of(8, lambda i: touch_s.at[i, 1], lambda i: touch_r.at[i, 1], other)
+    for copy in corners + edges:
         copy.wait_recv()
 
-    sums = []
-    for k, (start, size) in enumerate(chunks):
-        sl = pl.ds(start, size)
+    def rows_of(size):
+        return lax.broadcasted_iota(jnp.int32, (size,) + xv.shape[2:], 1)
+
+    sums, passes = [], []
+    for k in range(max(EARLY, LATE)):
+        if k < LATE:
+            sl = pl.ds(*late_chunks[k])
+            parts[k].wait_recv()
+            passes.append(
+                send(part.at[sl], beyond.at[sl], pass_ss.at[k], pass_rs.at[k], (source, n))
+            )
+        if k < EARLY:
+            start, size = early_chunks[k]
+            sl, row = pl.ds(start, size), rows_of(size)
+            coeff = c_ref[sl]
+            square, twice = coeff * coeff, 2.0 * coeff
+            own_near, own_far = xv[sl, near], xv[sl, far]
+            plane = in_plane(
+                own_near, edge_r[0, sl][:, None, :], edge_r[1, sl][:, None, :], row, coeff
+            )
+            raws[k].wait_recv()
+            raw_near, raw_far = raw[sl, far], raw[sl, near]
+            sums_s[sl, far] = twice * plane + square * (own_far + raw_near)
+            plane = in_plane(
+                raw_near, corner_r[0, sl][:, None, :], corner_r[1, sl][:, None, :], row, coeff
+            )
+            sums_s[sl, near] = twice * plane + square * (own_near + raw_far)
+            sums.append(
+                send(sums_s.at[sl], sums_r.at[sl], sums_ss.at[k], sums_rs.at[k], (partner, n))
+            )
+
+    for copy in rests:
+        copy.wait_recv()
+    for start, size in pieces(nspec, EARLY + LATE):
+        sl, row = pl.ds(start, size), rows_of(size)
         coeff = c_ref[sl]
-        square = coeff * coeff
-        row = lax.broadcasted_iota(jnp.int32, (size,) + xv.shape[2:], 1)
-        low, high = halo_r[0, sl], halo_r[1, sl]
+        square, twice = coeff * coeff, 2.0 * coeff
+
+        def halo(low, high, low_inner, high_inner):
+            low, high, low_inner, high_inner = (
+                v[:, None, :] for v in (low, high, low_inner, high_inner)
+            )
+            tile = jnp.where(row == 0, high, high_inner)
+            return jnp.where(row == cy - 1, low, jnp.where(row == cy - 2, low_inner, tile))
+
+        own = xv[sl, near], xv[sl, far]
         halos = (
-            jnp.where(row < half, high, low),
-            pltpu.roll(jnp.where(row < half, low, high), half, 1),
+            halo(edge_r[0, sl], edge_r[1, sl], rest_r[0, 1, sl], rest_r[1, 1, sl]),
+            halo(rest_r[0, 0, sl], rest_r[1, 0, sl], rest_r[0, 2, sl], rest_r[1, 2, sl]),
         )
-        own_near, own_far = xv[sl, near], xv[sl, far]
-        halo_near = jnp.where(near == 0, halos[0], halos[1])
-        beyond = square * own_far + (2.0 * coeff) * in_plane(
-            own_near, *rolled(halo_near), row, coeff
-        )
-        within = square * own_near
-        raws[k].wait_recv()
-        raw_near, raw_far = raw[sl, far], raw[sl, near]
-        plane = in_plane(
-            raw_near, corner_r[0, sl][:, None, :], corner_r[1, sl][:, None, :], row, coeff
-        )
-        sums_s[sl, near] = within + square * raw_far + (2.0 * coeff) * plane
-        sums_s[sl, far] = beyond + square * raw_near
-        sums.append(
-            send(sums_s.at[sl], sums_r.at[sl], sums_ss.at[k], sums_rs.at[k], (partner, n))
-        )
-        for i in range(2):
-            mine, other = xv[sl, i], xv[sl, 1 - i]
-            centre = in_plane(mine, *rolled(halos[i]), row, coeff) + (2.0 * coeff) * other
-            edge = in_plane(halos[i], *rolled(mine), row, coeff) + (2.0 * coeff) * halos[1 - i]
-            out_ref[sl, i] = in_plane(centre, *rolled(edge), row, coeff) + (2.0 * square) * mine
-
-    for k, (start, size) in enumerate(chunks):
-        sl = pl.ds(start, size)
-        sums[k].wait_recv()
-        out_ref[sl] = out_ref[sl] + sums_r[sl]
-    for copy in sides + raws + sums:
+        for i, at in enumerate((near, far)):
+            mine, side = own[i], halos[i]
+            centre = in_plane(mine, *rolled(side), row, coeff) + twice * own[1 - i]
+            edge = in_plane(side, *rolled(mine), row, coeff) + twice * halos[1 - i]
+            out_ref[sl, at] = in_plane(centre, *rolled(edge), row, coeff) + 2.0 * square * mine
+
+    for copy in touches:
+        copy.wait_recv()
+    for k in range(max(EARLY, LATE)):
+        if k < EARLY:
+            sl = pl.ds(*early_chunks[k])
+            sums[k].wait_recv()
+            out_ref[sl] = out_ref[sl] + sums_r[sl]
+        if k < LATE:
+            start, size = late_chunks[k]
+            sl, to, row = pl.ds(start, size), pl.ds(early + start, size), rows_of(size)
+            coeff = c_ref[to]
+            square, twice = coeff * coeff, 2.0 * coeff
+            close, second = part[sl, far], part[sl, near]
+            plane = twice * in_plane(
+                close, touch_r[0, 0, sl][:, None, :], touch_r[1, 0, sl][:, None, :], row, coeff
+            )
+            passes[k].wait_recv()
+            ahead, third = beyond[sl, near], beyond[sl, far]
+            out_ref[to, near] = out_ref[to, near] + plane + square * (second + ahead)
+            plane = twice * in_plane(
+                ahead, touch_r[0, 1, sl][:, None, :], touch_r[1, 1, sl][:, None, :], row, coeff
+            )
+            out_ref[to, far] = out_ref[to, far] + plane + square * (third + close)
+    for copy in corners + edges + rests + touches + raws + parts + sums + passes:
         copy.wait_send()
 
 
@@ -200,6 +260,7 @@
     smem = pl.BlockSpec(memory_space=pltpu.SMEM)
     coeff = jnp.broadcast_to(spreading_number[:, None, None], (nspec, 1, height))
     dma = pltpu.SemaphoreType.DMA
+    early = nspec // 16 * 8
     mixed = pl.pallas_call(
         functools.partial(exchange, n_wide, n_narrow),
         out_shape=jax.ShapeDtypeStruct(shape, f32),
@@ -207,20 +268,16 @@
         out_specs=vmem,
         scratch_shapes=[
             pltpu.VMEM(shape, f32),
-            pltpu.VMEM(shape, f32),
-            pltpu.VMEM((2, nspec, height), f32),
-            pltpu.VMEM((2, nspec, height), f32),
-            pltpu.VMEM((2, nspec, cy, height), f32),
-            pltpu.VMEM((2, nspec, cy, height), f32),
-            pltpu.VMEM(shape, f32),
-            pltpu.VMEM(shape, f32),
+            *[pltpu.VMEM((early,) + shape[1:], f32)] * 3,
+            *[pltpu.VMEM((nspec - early,) + shape[1:], f32)] * 2,
+            *[pltpu.VMEM((2, early, height), f32)] * 2,
+            *[pltpu.VMEM((2, 2, nspec - early, height), f32)] * 2,
+            *[pltpu.VMEM((2, nspec, height), f32)] * 2,
+            *[pltpu.VMEM((2, 3, nspec, height), f32)] * 2,
             dma(()),
-            dma((CHUNKS,)),
-            dma((CHUNKS,)),
-            dma((CHUNKS,)),
-            dma((CHUNKS,)),
-            dma((4,)),
-            dma((4,)),
+            *[dma((EARLY,))] * 4,
+            *[dma((LATE,))] * 4,
+            *[dma((10,))] * 2,
         ],
         compiler_params=pltpu.CompilerParams(
             collective_id=0, has_side_effects=True, vmem_limit_bytes=32 * 2**20

time: 31 us -> 27.2 us (0.88)
  Pallas kernels: 26.6 us -> 22.8 us
    pallas_call x1, Pallas kernels: 23.5 us -> 19.7 us  [shards(): pl.pallas_call(functools.partial(exchange, n_wide, n_narrow), out_shape=j...]
where the time goes in v3:
time: 27.2 us; the launch traced here: 27 us
  Pallas kernels  22.8 us (84%)
  local copies, waits for them, and re-layouts  3.1 us (11%)
  other arithmetic  0.95 us (3%)
    pallas_call x1, Pallas kernels, shards(): pl.pallas_call(functools.partial(exchange, n_wide, n_narrow), out_shape=j...  19.7 us
    pallas_call x1, Pallas kernels, shards(): pl.pallas_call(reaction, out_shape=jax.ShapeDtypeStruct((nspec * cx * cy,...  3.09 us
    unnamed x12, local copies, waits for them, and re-layouts  1.92 us
    convert_element_type x1, other arithmetic, shards(): incoming = jnp.pad(incoming_stoichiometry.astype(bf16), ((0, more), (0, 0)))  0.93 us
    pad x1, local copies, waits for them, and re-layouts, shards(): jnp.pad(natural_exponent_scale, (0, more))[:, None]  0.7 us

profile of v3, /device:TPU:0, one launch (start us, length us, event | category | flops | bytes accessed | tf_op | source)
XLA Modules:
  0.0 27.0 jit_solution(17039157297275675119)
XLA Ops:
  0.0 0.0 copy-start.4
  0.0 0.7 %pad.25 = f32[336]{0:T(512)S(1)} pad(f32[325]{0:T(512)} %param.12, f32[]{:T(128)} %constant.3.clone.1), padding=0_11 | pad | bytes 2648 | tf_op jit(solution)/shard_map/jit(_pad)/pad | solution.py:315
  0.7 0.0 copy-done.4
  0.7 0.0 copy-start.5
  0.7 0.6 %copy-done.5 = f32[53]{0:T(128)S(1)} copy-done((f32[53]{0:T(128)S(1)}, f32[53]{0:T(128)}, u32[]{:S(2)}) %copy-start.5) | copy-done | bytes 236
  1.4 0.1 broadcast_in_dim.12.c_ref
  1.5 0.0 copy-start.3
  1.5 0.9 %convert_element_type.17 = bf16[325,53]{0,1:T(8,128)(2,1)S(1)} convert(s32[325,53]{0,1:T(8,128)} %param.14) | non-fusion elementwise | flops 17225 | bytes 103350 | tf_op jit(solution)/shard_map/convert_element_type | solution.py:291
  2.4 0.0 copy-done.3
  2.5 0.0 copy-start
  2.5 0.1 copy.12.logs_ref
  2.7 0.1 broadcast_in_dim.16.energy_ref
  2.8 0.1 broadcast_in_dim.15.scale_ref
  2.9 0.6 %copy-done = f32[53,2,8,128]{3,2,1,0:T(8,128)S(1)} copy-done((f32[53,2,8,128]{3,2,1,0:T(8,128)S(1)}, f32[53,2,8,128]{3,2,1,0:T(8,128)}, u32[]{:S(2)}) %copy-start) | copy-done | bytes 434200
  3.5 0.0 copy-start.1
  3.5 19.7 %exchange.1 = f32[53,2,8,128]{3,2,1,0:T(8,128)S(1)} custom-call(f32[53,2,8,128]{3,2,1,0:T(8,128)S(1)} %copy-done, f32[53,1,128]{2,1,0:T(1,128)S(1)} %broadcast_in_dim.12.c_ref), custom_call_target="tpu_custom_call" | custom-call | tf_op jit(solution)/shard_map/exchange/pallas_call | solution.py:264
  23.2 0.0 copy-start.2
  23.2 0.0 copy-done.1
  23.2 0.7 %copy-done.2 = s32[2,8]{1,0:T(2,128)S(1)} copy-done((s32[2,8]{1,0:T(2,128)S(1)}, s32[2,8]{1,0:T(2,128)}, u32[]{:S(2)}) %copy-start.2) | copy-done | bytes 88
  23.9 3.1 %reaction.1 = f32[848,128]{1,0:T(8,128)} custom-call(s32[2,8]{1,0:T(2,128)S(1)} %copy-done.2, f32[848,128]{1,0:T(8,128)S(1)} %bitcast.6, f32[16,128]{1,0:T(8,128)S(1)} %bitcast.7, f32[336,1]{1,0:T(8,128)S(1)} %broadcast_in_dim.15.scale_ref, f32[336,1]{1,0:T(8,128)S(1)} %broadcast_in_dim.16.energy_ref, bf16[336,128]{1,0:T(8,128)(2,1)S(1)} %copy.12.logs_ref, ...), custom_call_target="tpu_custom_call" | custom-call | tf_op jit(solution)/shard_map/reaction/pallas_call | solution.py:298
  (6 shorter events, 0.1 us)
Async XLA Ops:
  0.0 0.7 %copy-start.4 = (f32[325]{0:T(512)S(1)}, f32[325]{0:T(512)}, u32[]{:S(2)}) copy-start(f32[325]{0:T(512)} %param.13) | copy-start | bytes 3904
  0.7 0.7 %copy-start.5 = (f32[53]{0:T(128)S(1)}, f32[53]{0:T(128)}, u32[]{:S(2)}) copy-start(f32[53]{0:T(128)} %param.11) | copy-start | bytes 640
  1.5 1.0 %copy-start.3 = (s32[325,53]{0,1:T(8,128)S(1)}, s32[325,53]{0,1:T(8,128)}, u32[]{:S(2)}) copy-start(s32[325,53]{0,1:T(8,128)} %param.15) | copy-start | bytes 206704
  2.5 1.0 %copy-start = (f32[53,2,8,128]{3,2,1,0:T(8,128)S(1)}, f32[53,2,8,128]{3,2,1,0:T(8,128)}, u32[]{:S(2)}) copy-start(f32[53,2,8,128]{3,2,1,0:T(8,128)} %x_ref.1) | copy-start | bytes 1302532
  3.5 19.7 %copy-start.1 = (f32[2,8,128]{2,1,0:T(8,128)S(1)}, f32[2,8,128]{2,1,0:T(8,128)}, u32[]{:S(2)}) copy-start(f32[2,8,128]{2,1,0:T(8,128)} %param.9) | copy-start | bytes 24580
  23.2 0.7 %copy-start.2 = (s32[2,8]{1,0:T(2,128)S(1)}, s32[2,8]{1,0:T(2,128)}, u32[]{:S(2)}) copy-start(s32[2,8]{1,0:T(2,128)} %marks_ref.1) | copy-start | bytes 196

commit v4 on v3

--- a/solution.py
+++ b/solution.py
@@ -30,8 +30,44 @@
     return pltpu.roll(tile, 1, 1), pltpu.roll(tile, tile.shape[1] - 1, 1)
 
 
+def three_parts(values):
+    parts = []
+    for _ in range(3):
+        parts.append(values.astype(jnp.bfloat16).astype(jnp.float32))
+        values = values - parts[-1]
+    return parts
+
+
+def rows_by_index(shape, rows):
+    index = lax.broadcasted_iota(jnp.int32, shape, 0)
+    block = jnp.zeros(shape, jnp.float32)
+    for i, row in enumerate(rows):
+        block = jnp.where(index == i, row, block)
+    return block
+
+
+def prepare(scale_ref, energy_ref, incoming_ref, outgoing_ref, work, logs_ref, sums_ref):
+    nspec, nreact = incoming_ref.shape
+    room, pad = logs_ref.shape[1] // 4, sums_ref.shape[0] // 2
+    rows = logs_ref.shape[0]
+    incoming = incoming_ref[...].astype(jnp.float32)
+    work[...] = jnp.zeros_like(work)
+    work[0:nspec, 0:nreact] = outgoing_ref[...].astype(jnp.float32)
+    work[pad : pad + nspec, 0:nreact] = incoming
+    sums_ref[...] = work[0 : 2 * pad, 0:rows].astype(jnp.bfloat16)
+    work[...] = jnp.zeros_like(work)
+    work[0:nspec, 0:nreact] = incoming
+    work[room : room + nspec, 0:nreact] = incoming
+    a, e = three_parts(scale_ref[...][None]), three_parts(-energy_ref[...][None])
+    extra = (a[0], a[1], a[2], e[0], e[0], e[1], e[1], e[0], e[2])
+    work[2 * room : 2 * room + 16, 0:nreact] = rows_by_index((16, nreact), extra)
+    logs_ref[...] = work[...].T[0:rows].astype(jnp.bfloat16)
+
+
 def exchange(
-    n_wide, n_narrow, x_ref, c_ref, out_ref, xv, raw, sums_s, sums_r, part, beyond,
+    n_wide, n_narrow, x_ref, coeff_hbm, marks_hbm, scale_hbm, energy_hbm, incoming_hbm,
+    outgoing_hbm, out_ref, marks_ref, logs_ref, sums_ref, coeff_ref, scale_ref, energy_ref,
+    incoming_ref, outgoing_ref, work, c_ref, load_sem, xv, raw, sums_s, sums_r, part, beyond,
     corner_s, corner_r, touch_s, touch_r, edge_s, edge_r, rest_s, rest_r, local_sem,
     raw_ss, raw_rs, sums_ss, sums_rs, part_ss, part_rs, pass_ss, pass_rs, side_ss, side_rs,
 ):
@@ -49,6 +85,15 @@
 
     load = pltpu.make_async_copy(x_ref, xv, local_sem)
     load.start()
+    loads = [
+        pltpu.make_async_copy(src, dst, load_sem.at[i])
+        for i, (src, dst) in enumerate((
+            (coeff_hbm, coeff_ref), (marks_hbm, marks_ref), (scale_hbm, scale_ref),
+            (energy_hbm, energy_ref), (incoming_hbm, incoming_ref), (outgoing_hbm, outgoing_ref),
+        ))
+    ]
+    for copy in loads:
+        copy.start()
     barrier = pltpu.get_barrier_semaphore()
     greeted = [(w, left), (w, right)]
     greeted += [(a, b) for a in (source, partner) for b in (n, left, right)]
@@ -98,6 +143,11 @@
     rests = sides_of(4, lambda i: rest_s.at[i], lambda i: rest_r.at[i], w)
     touches = sides_of(6, lambda i: touch_s.at[i, 0], lambda i: touch_r.at[i, 0], partner)
     touches += sides_of(8, lambda i: touch_s.at[i, 1], lambda i: touch_r.at[i, 1], other)
+    for copy in loads:
+        copy.wait()
+    for i in range(nspec):
+        c_ref[i] = jnp.full(c_ref.shape[1:], coeff_ref[0, i], jnp.float32)
+    prepare(scale_ref, energy_ref, incoming_ref, outgoing_ref, work, logs_ref, sums_ref)
     for copy in corners + edges:
         copy.wait_recv()
 
@@ -190,13 +240,13 @@
 
 
 def reaction(
-    marks_ref, mixed_ref, heat_ref, scale_ref, energy_ref, logs_ref, sums_ref, out_ref,
+    marks_ref, mixed_ref, heat_ref, logs_ref, sums_ref, out_ref,
     picked, temps, stacked, slots,
 ):
     nspec = mixed_ref.shape[0] // heat_ref.shape[0]
     stacks, height = heat_ref.shape
     per_row = marks_ref.shape[1]
-    room = stacked.shape[0] // 2
+    room = stacked.shape[0] // 4
     pad = sums_ref.shape[0] // 2
     out_ref[...] = mixed_ref[...]
     for k in range(BURN_MAX):
@@ -215,13 +265,16 @@
         picked[:, cells] = mixed_ref[pl.ds(slots[k], nspec, stride=stacks), :]
         temps[:, cells] = heat_ref[pl.ds(slots[k], 1), :]
     stacked[...] = jnp.zeros_like(stacked)
-    base = scale_ref[...] - energy_ref[...] * (1.0 / temps[...])
+    t, one = three_parts(1.0 / temps[...]), jnp.ones(temps.shape, jnp.float32)
+    extra = (one, one, one, t[0], t[1], t[0], t[1], t[2], t[0])
+    extra = rows_by_index((16, temps.shape[1]), extra)
+    stacked[2 * room : 2 * room + 16, :] = extra.astype(jnp.bfloat16)
     values = picked[...]
     for substep in range(2):
         high, low = two_parts(jnp.log(values))
         stacked[0:nspec, :] = high
         stacked[room : room + nspec, :] = low
-        expo = base + jnp.dot(logs_ref[...], stacked[...], preferred_element_type=jnp.float32)
+        expo = jnp.dot(logs_ref[...], stacked[...], preferred_element_type=jnp.float32)
         high, low = two_parts(jnp.exp(expo))
         total = jnp.dot(sums_ref[...], high, preferred_element_type=jnp.float32)
         total = total + jnp.dot(sums_ref[...], low, preferred_element_type=jnp.float32)
@@ -258,15 +311,28 @@
     f32, bf16 = jnp.float32, jnp.bfloat16
     vmem = pl.BlockSpec(memory_space=pltpu.VMEM)
     smem = pl.BlockSpec(memory_space=pltpu.SMEM)
-    coeff = jnp.broadcast_to(spreading_number[:, None, None], (nspec, 1, height))
+    hbm = pl.BlockSpec(memory_space=pltpu.HBM)
+    room, rows = round_up(nspec, 64), round_up(nreact, 16)
+    pad, wide = round_up(nspec, 8), round_up(nreact, 128)
     dma = pltpu.SemaphoreType.DMA
     early = nspec // 16 * 8
-    mixed = pl.pallas_call(
+    mixed, marks, logs_mat, sums_mat = pl.pallas_call(
         functools.partial(exchange, n_wide, n_narrow),
-        out_shape=jax.ShapeDtypeStruct(shape, f32),
-        in_specs=[pl.BlockSpec(memory_space=pl.ANY), vmem],
-        out_specs=vmem,
+        out_shape=[
+            jax.ShapeDtypeStruct(shape, f32),
+            jax.ShapeDtypeStruct(ignited_stacks.shape, jnp.int32),
+            jax.ShapeDtypeStruct((rows, 4 * room), bf16),
+            jax.ShapeDtypeStruct((2 * pad, rows), bf16),
+        ],
+        in_specs=[hbm] * 7,
+        out_specs=[vmem] * 4,
         scratch_shapes=[
+            pltpu.SMEM((1, nspec), f32),
+            *[pltpu.VMEM((nreact,), f32)] * 2,
+            *[pltpu.VMEM((nspec, nreact), jnp.int32)] * 2,
+            pltpu.VMEM((4 * room, wide), f32),
+            pltpu.VMEM((nspec, 1, height), f32),
+            dma((6,)),
             pltpu.VMEM(shape, f32),
             *[pltpu.VMEM((early,) + shape[1:], f32)] * 3,
             *[pltpu.VMEM((nspec - early,) + shape[1:], f32)] * 2,
@@ -280,40 +346,37 @@
             *[dma((10,))] * 2,
         ],
         compiler_params=pltpu.CompilerParams(
-            collective_id=0, has_side_effects=True, vmem_limit_bytes=32 * 2**20
+            collective_id=0, has_side_effects=True, vmem_limit_bytes=53 * 2**20
         ),
         name="exchange",
-    )(chemical_fractions, coeff)
-
-    room, rows = round_up(nspec, 64), round_up(nreact, 16)
-    pad = round_up(nspec, 8)
-    more = rows - nreact
-    incoming = jnp.pad(incoming_stoichiometry.astype(bf16), ((0, more), (0, 0)))
-    outgoing = jnp.pad(outgoing_stoichiometry.astype(bf16), ((0, more), (0, 0)))
-    logs_mat = jnp.tile(jnp.pad(incoming, ((0, 0), (0, room - nspec))), (1, 2))
-    sums_mat = jnp.concatenate(
-        [jnp.pad(m, ((0, 0), (0, pad - nspec))) for m in (outgoing, incoming)], axis=1
-    ).T
+    )(
+        chemical_fractions,
+        spreading_number[None],
+        ignited_stacks,
+        natural_exponent_scale,
+        arrhenius_energy,
+        incoming_stoichiometry.T,
+        outgoing_stoichiometry.T,
+    )
+
     cells = BURN_MAX * height
     updated = pl.pallas_call(
         reaction,
         out_shape=jax.ShapeDtypeStruct((nspec * cx * cy, height), f32),
-        in_specs=[smem] + [vmem] * 6,
+        in_specs=[smem] + [vmem] * 4,
         out_specs=vmem,
         scratch_shapes=[
             pltpu.VMEM((nspec, cells), f32),
             pltpu.VMEM((1, cells), f32),
-            pltpu.VMEM((2 * room, cells), bf16),
+            pltpu.VMEM((4 * room, cells), bf16),
             pltpu.SMEM((BURN_MAX,), jnp.int32),
         ],
         compiler_params=pltpu.CompilerParams(vmem_limit_bytes=32 * 2**20),
         name="reaction",
     )(
-        ignited_stacks,
+        marks,
         mixed.reshape(nspec * cx * cy, height),
         thermal_state.reshape(cx * cy, height),
-        jnp.pad(natural_exponent_scale, (0, more))[:, None],
-        jnp.pad(arrhenius_energy, (0, more))[:, None],
         logs_mat,
         sums_mat,
     )

time: 27.2 us -> 26.2 us (0.963)
  other arithmetic: 0.95 us -> 0 us
    unnamed x12 -> x14, local copies, waits for them, and re-layouts: 1.92 us -> 3.18 us
    convert_element_type x2 -> x0, other arithmetic: 0.94 us -> none  [the longest x1 0.93 us: shards(): incoming = jnp.pad(incoming_stoichiometry.astype(bf16), ((0, more), (0, 0)))]
    pad x4 -> x0, local copies, waits for them, and re-layouts: 0.72 us -> none  [the longest x1 0.7 us: shards(): jnp.pad(natural_exponent_scale, (0, more))[:, None]]
    broadcast_in_dim x3 -> x0, local copies, waits for them, and re-layouts: 0.32 us -> none  [the longest x1 0.11 us: shards(): jnp.broadcast_to(spreading_number[:, None, None], (nspec, 1, height))]
where the time goes in v4:
time: 26.2 us; the launch traced here: 25.9 us
  Pallas kernels  22.7 us (87%)
  local copies, waits for them, and re-layouts  3.18 us (12%)
    pallas_call x1, Pallas kernels, shards(): pl.pallas_call(functools.partial(exchange, n_wide, n_narrow), out_shape=[...  19.8 us
    unnamed x14, local copies, waits for them, and re-layouts  3.18 us
    pallas_call x1, Pallas kernels, shards(): pl.pallas_call(reaction, out_shape=jax.ShapeDtypeStruct((nspec * cx * cy,...  2.96 us

profile of v4, /device:TPU:0, one launch (start us, length us, event | category | flops | bytes accessed | tf_op | source)
XLA Modules:
  0.0 25.9 jit_solution(9589197971165690286)
XLA Ops:
  0.0 0.0 copy-start.4
  0.0 0.0 copy-start.3
  0.0 0.0 copy-start.5
  0.0 0.0 copy-start.6
  0.0 0.7 %copy-done.4 = f32[325]{0:T(512)S(1)} copy-done((f32[325]{0:T(512)S(1)}, f32[325]{0:T(512)}, u32[]{:S(2)}) %copy-start.4) | copy-done | bytes 1324
  0.7 0.0 copy-done.3
  0.7 0.0 copy-done.5
  0.7 0.0 copy-done.6
  0.7 0.0 copy-start
  0.7 0.9 %copy-done = s32[325,53]{0,1:T(8,128)S(1)} copy-done((s32[325,53]{0,1:T(8,128)S(1)}, s32[325,53]{0,1:T(8,128)}, u32[]{:S(2)}) %copy-start) | copy-done | bytes 68924
  1.6 0.0 copy-start.1
  1.6 0.9 %copy-done.1 = s32[325,53]{0,1:T(8,128)S(1)} copy-done((s32[325,53]{0,1:T(8,128)S(1)}, s32[325,53]{0,1:T(8,128)}, u32[]{:S(2)}) %copy-start.1) | copy-done | bytes 68924
  2.5 19.8 %exchange.1 = (f32[53,2,8,128]{3,2,1,0:T(8,128)S(1)}, s32[2,8]{1,0:T(2,128)S(1)}, bf16[336,256]{1,0:T(8,128)(2,1)S(1)}, bf16[112,336]{1,0:T(8,128)(2,1)S(1)}) custom-call(f32[53,2,8,128]{3,2,1,0:T(8,128)} %x_ref.1, f32[1,53]{1,0:T(1,128)S(1)} %bitcast.10, s32[2,8]{1,0:T(2,128)S(1)} %copy-done.5, f32[325]{0:T(512)S(1)} %copy-done.3, f32[325]{0:T(512)S(1)} %copy-done.4, ...), custom_call_target="tpu_custom_call" | custom-call | tf_op jit(solution)/shard_map/exchange/pallas_call | solution.py:319
  22.3 0.0 copy-start.2
  22.3 0.7 %copy-done.2 = f32[2,8,128]{2,1,0:T(8,128)S(1)} copy-done((f32[2,8,128]{2,1,0:T(8,128)S(1)}, f32[2,8,128]{2,1,0:T(8,128)}, u32[]{:S(2)}) %copy-start.2) | copy-done | bytes 8216
  23.0 3.0 %reaction.1 = f32[848,128]{1,0:T(8,128)} custom-call(s32[2,8]{1,0:T(2,128)S(1)} %get-tuple-element.9.marks_ref, f32[848,128]{1,0:T(8,128)S(1)} %bitcast.6, f32[16,128]{1,0:T(8,128)S(1)} %bitcast.9, bf16[336,256]{1,0:T(8,128)(2,1)S(1)} %get-tuple-element.11.logs_ref, bf16[112,336]{1,0:T(8,128)(2,1)S(1)} %get-tuple-element.12.sums_ref), custom_call_target="tpu_custom_call" | custom-call | tf_op jit(solution)/shard_map/reaction/pallas_call | solution.py:363
Async XLA Ops:
  0.0 0.7 %copy-start.4 = (f32[325]{0:T(512)S(1)}, f32[325]{0:T(512)}, u32[]{:S(2)}) copy-start(f32[325]{0:T(512)} %energy_hbm.1) | copy-start | bytes 3904
  0.0 0.7 %copy-start.3 = (f32[325]{0:T(512)S(1)}, f32[325]{0:T(512)}, u32[]{:S(2)}) copy-start(f32[325]{0:T(512)} %scale_hbm.1) | copy-start | bytes 3904
  0.0 0.7 %copy-start.5 = (s32[2,8]{1,0:T(2,128)S(1)}, s32[2,8]{1,0:T(2,128)}, u32[]{:S(2)}) copy-start(s32[2,8]{1,0:T(2,128)} %marks_hbm.1) | copy-start | bytes 196
  0.0 0.7 %copy-start.6 = (f32[53]{0:T(128)S(1)}, f32[53]{0:T(128)}, u32[]{:S(2)}) copy-start(f32[53]{0:T(128)} %param.11) | copy-start | bytes 640
  0.7 0.9 %copy-start = (s32[325,53]{0,1:T(8,128)S(1)}, s32[325,53]{0,1:T(8,128)}, u32[]{:S(2)}) copy-start(s32[325,53]{0,1:T(8,128)} %param.14) | copy-start | bytes 206704
  1.6 0.9 %copy-start.1 = (s32[325,53]{0,1:T(8,128)S(1)}, s32[325,53]{0,1:T(8,128)}, u32[]{:S(2)}) copy-start(s32[325,53]{0,1:T(8,128)} %param.15) | copy-start | bytes 206704
  22.3 0.7 %copy-start.2 = (f32[2,8,128]{2,1,0:T(8,128)S(1)}, f32[2,8,128]{2,1,0:T(8,128)}, u32[]{:S(2)}) copy-start(f32[2,8,128]{2,1,0:T(8,128)} %param.9) | copy-start | bytes 24580

commit v5 on v4

--- a/solution.py
+++ b/solution.py
@@ -65,8 +65,8 @@
 
 
 def exchange(
-    n_wide, n_narrow, x_ref, coeff_hbm, marks_hbm, scale_hbm, energy_hbm, incoming_hbm,
-    outgoing_hbm, out_ref, marks_ref, logs_ref, sums_ref, coeff_ref, scale_ref, energy_ref,
+    n_wide, n_narrow, x_ref, coeff_hbm, scale_hbm, energy_hbm, incoming_hbm,
+    outgoing_hbm, out_hbm, logs_hbm, sums_hbm, out_ref, logs_ref, sums_ref, store_sem, coeff_ref, scale_ref, energy_ref,
     incoming_ref, outgoing_ref, work, c_ref, load_sem, xv, raw, sums_s, sums_r, part, beyond,
     corner_s, corner_r, touch_s, touch_r, edge_s, edge_r, rest_s, rest_r, local_sem,
     raw_ss, raw_rs, sums_ss, sums_rs, part_ss, part_rs, pass_ss, pass_rs, side_ss, side_rs,
@@ -88,8 +88,8 @@
     loads = [
         pltpu.make_async_copy(src, dst, load_sem.at[i])
         for i, (src, dst) in enumerate((
-            (coeff_hbm, coeff_ref), (marks_hbm, marks_ref), (scale_hbm, scale_ref),
-            (energy_hbm, energy_ref), (incoming_hbm, incoming_ref), (outgoing_hbm, outgoing_ref),
+            (coeff_hbm, coeff_ref), (scale_hbm, scale_ref), (energy_hbm, energy_ref),
+            (incoming_hbm, incoming_ref), (outgoing_hbm, outgoing_ref),
         ))
     ]
     for copy in loads:
@@ -148,6 +148,14 @@
     for i in range(nspec):
         c_ref[i] = jnp.full(c_ref.shape[1:], coeff_ref[0, i], jnp.float32)
     prepare(scale_ref, energy_ref, incoming_ref, outgoing_ref, work, logs_ref, sums_ref)
+    stores = []
+
+    def store(src, dst):
+        stores.append(pltpu.make_async_copy(src, dst, store_sem.at[len(stores)]))
+        stores[-1].start()
+
+    store(logs_ref, logs_hbm)
+    store(sums_ref, sums_hbm)
     for copy in corners + edges:
         copy.wait_recv()
 
@@ -214,6 +222,7 @@
             sl = pl.ds(*early_chunks[k])
             sums[k].wait_recv()
             out_ref[sl] = out_ref[sl] + sums_r[sl]
+            store(out_ref.at[sl], out_hbm.at[sl])
         if k < LATE:
             start, size = late_chunks[k]
             sl, to, row = pl.ds(start, size), pl.ds(early + start, size), rows_of(size)
@@ -230,8 +239,11 @@
                 ahead, touch_r[0, 1, sl][:, None, :], touch_r[1, 1, sl][:, None, :], row, coeff
             )
             out_ref[to, far] = out_ref[to, far] + plane + square * (third + close)
+            store(out_ref.at[to], out_hbm.at[to])
     for copy in corners + edges + rests + touches + raws + parts + sums + passes:
         copy.wait_send()
+    for copy in stores:
+        copy.wait()
 
 
 def two_parts(values):
@@ -240,17 +252,27 @@
 
 
 def reaction(
-    marks_ref, mixed_ref, heat_ref, logs_ref, sums_ref, out_ref,
-    picked, temps, stacked, slots,
+    marks_hbm, mixed_hbm, heat_hbm, logs_hbm, sums_hbm, out_ref,
+    marks_ref, heat_ref, logs_ref, sums_ref, sems, picked, temps, stacked, slots,
 ):
-    nspec = mixed_ref.shape[0] // heat_ref.shape[0]
+    loads = [
+        pltpu.make_async_copy(src, dst, sems.at[i])
+        for i, (src, dst) in enumerate((
+            (marks_hbm, marks_ref), (heat_hbm, heat_ref), (mixed_hbm, out_ref),
+            (logs_hbm, logs_ref), (sums_hbm, sums_ref),
+        ))
+    ]
+    for copy in loads:
+        copy.start()
+    nspec = out_ref.shape[0] // heat_ref.shape[0]
     stacks, height = heat_ref.shape
     per_row = marks_ref.shape[1]
     room = stacked.shape[0] // 4
     pad = sums_ref.shape[0] // 2
-    out_ref[...] = mixed_ref[...]
+    stacked[...] = jnp.zeros_like(stacked)
     for k in range(BURN_MAX):
         slots[k] = 0
+    loads[0].wait()
     count = jnp.int32(0)
     for i in range(stacks):
         burning = marks_ref[i // per_row, i % per_row]
@@ -260,11 +282,12 @@
             slots[count] = i
 
         count = count + burning
+    for copy in loads[1:]:
+        copy.wait()
     for k in range(BURN_MAX):
         cells = pl.ds(k * height, height)
-        picked[:, cells] = mixed_ref[pl.ds(slots[k], nspec, stride=stacks), :]
+        picked[:, cells] = out_ref[pl.ds(slots[k], nspec, stride=stacks), :]
         temps[:, cells] = heat_ref[pl.ds(slots[k], 1), :]
-    stacked[...] = jnp.zeros_like(stacked)
     t, one = three_parts(1.0 / temps[...]), jnp.ones(temps.shape, jnp.float32)
     extra = (one, one, one, t[0], t[1], t[0], t[1], t[2], t[0])
     extra = rows_by_index((16, temps.shape[1]), extra)
@@ -310,29 +333,31 @@
     nreact = incoming_stoichiometry.shape[0]
     f32, bf16 = jnp.float32, jnp.bfloat16
     vmem = pl.BlockSpec(memory_space=pltpu.VMEM)
-    smem = pl.BlockSpec(memory_space=pltpu.SMEM)
     hbm = pl.BlockSpec(memory_space=pltpu.HBM)
     room, rows = round_up(nspec, 64), round_up(nreact, 16)
     pad, wide = round_up(nspec, 8), round_up(nreact, 128)
     dma = pltpu.SemaphoreType.DMA
     early = nspec // 16 * 8
-    mixed, marks, logs_mat, sums_mat = pl.pallas_call(
+    mixed, logs_mat, sums_mat = pl.pallas_call(
         functools.partial(exchange, n_wide, n_narrow),
         out_shape=[
             jax.ShapeDtypeStruct(shape, f32),
-            jax.ShapeDtypeStruct(ignited_stacks.shape, jnp.int32),
             jax.ShapeDtypeStruct((rows, 4 * room), bf16),
             jax.ShapeDtypeStruct((2 * pad, rows), bf16),
         ],
-        in_specs=[hbm] * 7,
-        out_specs=[vmem] * 4,
+        in_specs=[hbm] * 6,
+        out_specs=[hbm] * 3,
         scratch_shapes=[
+            pltpu.VMEM(shape, f32),
+            pltpu.VMEM((rows, 4 * room), bf16),
+            pltpu.VMEM((2 * pad, rows), bf16),
+            dma((EARLY + LATE + 2,)),
             pltpu.SMEM((1, nspec), f32),
             *[pltpu.VMEM((nreact,), f32)] * 2,
             *[pltpu.VMEM((nspec, nreact), jnp.int32)] * 2,
             pltpu.VMEM((4 * room, wide), f32),
             pltpu.VMEM((nspec, 1, height), f32),
-            dma((6,)),
+            dma((5,)),
             pltpu.VMEM(shape, f32),
             *[pltpu.VMEM((early,) + shape[1:], f32)] * 3,
             *[pltpu.VMEM((nspec - early,) + shape[1:], f32)] * 2,
@@ -346,13 +371,12 @@
             *[dma((10,))] * 2,
         ],
         compiler_params=pltpu.CompilerParams(
-            collective_id=0, has_side_effects=True, vmem_limit_bytes=53 * 2**20
+            collective_id=0, has_side_effects=True, vmem_limit_bytes=60 * 2**20
         ),
         name="exchange",
     )(
         chemical_fractions,
         spreading_number[None],
-        ignited_stacks,
         natural_exponent_scale,
         arrhenius_energy,
         incoming_stoichiometry.T,
@@ -363,18 +387,23 @@
     updated = pl.pallas_call(
         reaction,
         out_shape=jax.ShapeDtypeStruct((nspec * cx * cy, height), f32),
-        in_specs=[smem] + [vmem] * 4,
+        in_specs=[hbm] * 5,
         out_specs=vmem,
         scratch_shapes=[
+            pltpu.SMEM(ignited_stacks.shape, jnp.int32),
+            pltpu.VMEM((cx * cy, height), f32),
+            pltpu.VMEM((rows, 4 * room), bf16),
+            pltpu.VMEM((2 * pad, rows), bf16),
+            dma((5,)),
             pltpu.VMEM((nspec, cells), f32),
             pltpu.VMEM((1, cells), f32),
             pltpu.VMEM((4 * room, cells), bf16),
             pltpu.SMEM((BURN_MAX,), jnp.int32),
         ],
-        compiler_params=pltpu.CompilerParams(vmem_limit_bytes=32 * 2**20),
+        compiler_params=pltpu.CompilerParams(vmem_limit_bytes=60 * 2**20),
         name="reaction",
     )(
-        marks,
+        ignited_stacks,
         mixed.reshape(nspec * cx * cy, height),
         thermal_state.reshape(cx * cy, height),
         logs_mat,

time: 26.2 us -> 23.9 us (0.912)
  local copies, waits for them, and re-layouts: 3.18 us -> 0 us
  Pallas kernels: 22.7 us -> 23.7 us
    unnamed x14 -> x0, local copies, waits for them, and re-layouts: 3.18 us -> none
    pallas_call x1, Pallas kernels: 2.96 us -> 3.55 us  [shards(): pl.pallas_call(reaction, out_shape=jax.ShapeDtypeStruct((nspec * cx * cy,...]
    pallas_call x1, Pallas kernels: 19.8 us -> 20.2 us  [shards(): pl.pallas_call(functools.partial(exchange, n_wide, n_narrow), out_shape=[...]
where the time goes in v5:
time: 23.9 us; the launch traced here: 23.7 us
  Pallas kernels  23.7 us (99%)
    pallas_call x1, Pallas kernels, shards(): pl.pallas_call(functools.partial(exchange, n_wide, n_narrow), out_shape=[...  20.2 us
    pallas_call x1, Pallas kernels, shards(): pl.pallas_call(reaction, out_shape=jax.ShapeDtypeStruct((nspec * cx * cy,...  3.55 us

profile of v5, /device:TPU:0, one launch (start us, length us, event | category | flops | bytes accessed | tf_op | source)
XLA Modules:
  0.0 23.7 jit_solution(12054975040688499336)
XLA Ops:
  0.0 20.2 %exchange.1 = (f32[53,2,8,128]{3,2,1,0:T(8,128)}, bf16[336,256]{1,0:T(8,128)(2,1)}, bf16[112,336]{1,0:T(8,128)(2,1)}) custom-call(f32[53,2,8,128]{3,2,1,0:T(8,128)} %x_ref.1, f32[1,53]{1,0:T(1,128)} %bitcast.10, f32[325]{0:T(512)} %scale_hbm.1, f32[325]{0:T(512)} %energy_hbm.1, s32[53,325]{1,0:T(8,128)} %bitcast.7, s32[53,325]{1,0:T(8,128)} %bitcast.8), custom_call_target="tpu_custom_call" | custom-call | tf_op jit(solution)/shard_map/exchange/pallas_call | solution.py:341
  20.2 3.6 %reaction.1 = f32[848,128]{1,0:T(8,128)} custom-call(s32[2,8]{1,0:T(2,128)} %marks_hbm.1, f32[848,128]{1,0:T(8,128)} %bitcast.6, f32[16,128]{1,0:T(8,128)} %bitcast.9, bf16[336,256]{1,0:T(8,128)(2,1)} %get-tuple-element.9.logs_hbm, bf16[112,336]{1,0:T(8,128)(2,1)} %get-tuple-element.10.sums_hbm), custom_call_target="tpu_custom_call" | custom-call | tf_op jit(solution)/shard_map/reaction/pallas_call | solution.py:387

commit v6 on v5

--- a/solution.py
+++ b/solution.py
@@ -282,34 +282,47 @@
             slots[count] = i
 
         count = count + burning
-    for copy in loads[1:]:
-        copy.wait()
+    loads[1].wait()
     for k in range(BURN_MAX):
-        cells = pl.ds(k * height, height)
-        picked[:, cells] = out_ref[pl.ds(slots[k], nspec, stride=stacks), :]
-        temps[:, cells] = heat_ref[pl.ds(slots[k], 1), :]
+        temps[:, k * height : (k + 1) * height] = heat_ref[pl.ds(slots[k], 1), :]
     t, one = three_parts(1.0 / temps[...]), jnp.ones(temps.shape, jnp.float32)
     extra = (one, one, one, t[0], t[1], t[0], t[1], t[2], t[0])
     extra = rows_by_index((16, temps.shape[1]), extra)
     stacked[2 * room : 2 * room + 16, :] = extra.astype(jnp.bfloat16)
-    values = picked[...]
+    whole = nspec // 8 * 8
+    groups = [(0, whole)] + [(i, 1) for i in range(whole, nspec)]
+    for copy in loads[2:]:
+        copy.wait()
+    for k in range(BURN_MAX):
+        for first, size in groups:
+            stride = stacks if size > 1 else None
+            rows = pl.ds(slots[k] + first * stacks, size, stride=stride)
+            picked[first : first + size, k * height : (k + 1) * height] = out_ref[rows, :]
+    width = picked.shape[1] // 2
+    halves = [slice(i * width, (i + 1) * width) for i in range(2)]
+    values = [picked[:, cells] for cells in halves]
     for substep in range(2):
-        high, low = two_parts(jnp.log(values))
-        stacked[0:nspec, :] = high
-        stacked[room : room + nspec, :] = low
-        expo = jnp.dot(logs_ref[...], stacked[...], preferred_element_type=jnp.float32)
-        high, low = two_parts(jnp.exp(expo))
-        total = jnp.dot(sums_ref[...], high, preferred_element_type=jnp.float32)
-        total = total + jnp.dot(sums_ref[...], low, preferred_element_type=jnp.float32)
-        gain, loss = total[0:nspec], total[pad : pad + nspec]
-        values = values * (values + 0.5 * gain) / (values + 0.5 * loss)
-    picked[...] = values
+        for i, cells in enumerate(halves):
+            high, low = two_parts(jnp.log(values[i]))
+            stacked[0:nspec, cells] = high
+            stacked[room : room + nspec, cells] = low
+            expo = jnp.dot(logs_ref[...], stacked[:, cells], preferred_element_type=jnp.float32)
+            high, low = two_parts(jnp.exp(expo))
+            total = jnp.dot(sums_ref[...], high, preferred_element_type=jnp.float32)
+            total = total + jnp.dot(sums_ref[...], low, preferred_element_type=jnp.float32)
+            gain, loss = total[0:nspec], total[pad : pad + nspec]
+            values[i] = values[i] * (values[i] + 0.5 * gain) / (values[i] + 0.5 * loss)
+    for i, cells in enumerate(halves):
+        picked[:, cells] = values[i]
     for k in range(BURN_MAX):
 
         @pl.when(k < count)
         def _():
-            column = picked[:, k * height : (k + 1) * height]
-            out_ref[pl.ds(slots[k], nspec, stride=stacks), :] = column
+            for first, size in groups:
+                stride = stacks if size > 1 else None
+                rows = pl.ds(slots[k] + first * stacks, size, stride=stride)
+                column = picked[first : first + size, k * height : (k + 1) * height]
+                out_ref[rows, :] = column
 
 
 def round_up(value, step):

time: 23.9 us -> 24.2 us (1.013)
  Pallas kernels: 23.7 us -> 24 us
where the time goes in v6:
time: 24.2 us; the launch traced here: 24 us
  Pallas kernels  24 us (99%)
    pallas_call x1, Pallas kernels, shards(): pl.pallas_call(functools.partial(exchange, n_wide, n_narrow), out_shape=[...  20.2 us
    pallas_call x1, Pallas kernels, shards(): pl.pallas_call(reaction, out_shape=jax.ShapeDtypeStruct((nspec * cx * cy,...  3.79 us

profile of v6, /device:TPU:0, one launch (start us, length us, event | category | flops | bytes accessed | tf_op | source)
XLA Modules:
  0.0 24.0 jit_solution(10769901447669886471)
XLA Ops:
  0.0 20.2 %exchange.1 = (f32[53,2,8,128]{3,2,1,0:T(8,128)}, bf16[336,256]{1,0:T(8,128)(2,1)}, bf16[112,336]{1,0:T(8,128)(2,1)}) custom-call(f32[53,2,8,128]{3,2,1,0:T(8,128)} %x_ref.1, f32[1,53]{1,0:T(1,128)} %bitcast.10, f32[325]{0:T(512)} %scale_hbm.1, f32[325]{0:T(512)} %energy_hbm.1, s32[53,325]{1,0:T(8,128)} %bitcast.7, s32[53,325]{1,0:T(8,128)} %bitcast.8), custom_call_target="tpu_custom_call" | custom-call | tf_op jit(solution)/shard_map/exchange/pallas_call | solution.py:354
  20.2 3.8 %reaction.1 = f32[848,128]{1,0:T(8,128)} custom-call(s32[2,8]{1,0:T(2,128)} %marks_hbm.1, f32[848,128]{1,0:T(8,128)} %bitcast.6, f32[16,128]{1,0:T(8,128)} %bitcast.9, bf16[336,256]{1,0:T(8,128)(2,1)} %get-tuple-element.9.logs_hbm, bf16[112,336]{1,0:T(8,128)(2,1)} %get-tuple-element.10.sums_hbm), custom_call_target="tpu_custom_call" | custom-call | tf_op jit(solution)/shard_map/reaction/pallas_call | solution.py:400

commit v7 on v5

--- a/solution.py
+++ b/solution.py
@@ -8,8 +8,8 @@
 from jax.sharding import PartitionSpec as P
 
 BURN_MAX = 8
-EARLY = 3
-LATE = 3
+EARLY = 4
+LATE = 4
 MESH = pl.DeviceIdType.MESH
 
 

time: 23.9 us -> 24 us (level)
  no operation moved by 1% of the time
where the time goes in v7:
time: 24 us; the launch traced here: 23.8 us
  Pallas kernels  23.8 us (99%)
    pallas_call x1, Pallas kernels, shards(): pl.pallas_call(functools.partial(exchange, n_wide, n_narrow), out_shape=[...  20.3 us
    pallas_call x1, Pallas kernels, shards(): pl.pallas_call(reaction, out_shape=jax.ShapeDtypeStruct((nspec * cx * cy,...  3.55 us

profile of v7, /device:TPU:0, one launch (start us, length us, event | category | flops | bytes accessed | tf_op | source)
XLA Modules:
  0.0 23.8 jit_solution(3004774895019988675)
XLA Ops:
  0.0 20.3 %exchange.1 = (f32[53,2,8,128]{3,2,1,0:T(8,128)}, bf16[336,256]{1,0:T(8,128)(2,1)}, bf16[112,336]{1,0:T(8,128)(2,1)}) custom-call(f32[53,2,8,128]{3,2,1,0:T(8,128)} %x_ref.1, f32[1,53]{1,0:T(1,128)} %bitcast.10, f32[325]{0:T(512)} %scale_hbm.1, f32[325]{0:T(512)} %energy_hbm.1, s32[53,325]{1,0:T(8,128)} %bitcast.7, s32[53,325]{1,0:T(8,128)} %bitcast.8), custom_call_target="tpu_custom_call" | custom-call | tf_op jit(solution)/shard_map/exchange/pallas_call | solution.py:341
  20.3 3.6 %reaction.1 = f32[848,128]{1,0:T(8,128)} custom-call(s32[2,8]{1,0:T(2,128)} %marks_hbm.1, f32[848,128]{1,0:T(8,128)} %bitcast.6, f32[16,128]{1,0:T(8,128)} %bitcast.9, bf16[336,256]{1,0:T(8,128)(2,1)} %get-tuple-element.9.logs_hbm, bf16[112,336]{1,0:T(8,128)(2,1)} %get-tuple-element.10.sums_hbm), custom_call_target="tpu_custom_call" | custom-call | tf_op jit(solution)/shard_map/reaction/pallas_call | solution.py:387
